TPU v7x, 1024 devices: a whole 4x8x16 slice. The times are simulated.
1024 devices in a mesh: gy: 32 (over y_lo, z), gz: 32 (over y_hi, x, core).
Axes of the slice: x: 4, y: 8 (y_hi: 4, y_lo: 2; y = y_hi * 2 + y_lo), z: 16, core: 2. Of those that a mesh axis runs over, the one named last changes fastest.
Arguments:
- populations: float32 [19, 4, 256, 4096], P(None, None, 'gy', 'gz')
- marker_owner: int32 [524288, 1], P(('gy', 'gz')), may hold values from 0 to 31; in each aligned block of 512 rows (0 to 511, 512 to 1023, ...) at most 24 rows name the same one
- marker_cell: int32 [3, 524288], P(None, ('gy', 'gz')), may hold values from 0 to 126, as said below
- marker_frac: float32 [3, 524288], P(None, ('gy', 'gz')), may hold values from 0 to 1
- marker_speed: float32 [3, 524288], P(None, ('gy', 'gz')), may hold values from -0.2 to 0.2
- marker_count: int32 [1024], P(('gy', 'gz')), may hold values from 256 to 512
Outputs:
- populations_out: float32 [19, 4, 256, 4096], P(None, None, 'gy', 'gz')
- marker_force: float32 [3, 524288], P(None, ('gy', 'gz'))
Inputs may be any that keep to these rules, and one draw needn't show every extreme that they name: `marker_owner`: among the 512 markers of one device at most 24 name one owner. `marker_cell`: row 0 is below 4, row 1 below 7, row 2 below 127, so the stencil lies in the owner's block.
All inputs are finite; a program needn't handle non-finite values.
Results may differ from a plain program's by a relative error of at most 0.0003.
Values sent between devices are 32-bit elements; how exact they have to be, the bound alone decides.
No kernel may reach another device: no remote copies, remote signals or barrier semaphores. Data moves between devices by JAX's collectives and lax.ppermute only.
A program may use at most 64 MiB of HBM per device.

v0:
```python
import math

import jax
import jax.numpy as jnp
from jax import lax
from jax.experimental import pallas as pl
from jax.experimental.pallas import tpu as pltpu
from jax.sharding import PartitionSpec as P

INTERPRET = False

velocity_table = (
    (0, 0, 0),
    (1, 0, 0),
    (-1, 0, 0),
    (0, 1, 0),
    (0, -1, 0),
    (0, 0, 1),
    (0, 0, -1),
    (1, 1, 0),
    (-1, -1, 0),
    (1, -1, 0),
    (-1, 1, 0),
    (1, 0, 1),
    (-1, 0, -1),
    (1, 0, -1),
    (-1, 0, 1),
    (0, 1, 1),
    (0, -1, -1),
    (0, 1, -1),
    (0, -1, 1),
)
opposite = (0, 2, 1, 4, 3, 6, 5, 8, 7, 10, 9, 12, 11, 14, 13, 16, 15, 18, 17)
rising = tuple(i for i in range(19) if velocity_table[i][1] == 1)
falling = tuple(opposite[i] for i in rising)
level = tuple(i for i in range(19) if velocity_table[i][1] == 0)
ahead_z = tuple(i for i in range(19) if velocity_table[i][2] == 1)
back_z = tuple(opposite[i] for i in ahead_z)
tau_base = 0.52
smag_const = 0.17
ref_speed = 0.05

PLANES = 4
ROWS = 8
LANES = 128
SLOTS = 24
SHARE = 32
FEW = 4
SPARE = SLOTS - FEW
FIRST_SPARE = SHARE
FIRST_Z = SHARE + 2 * SPARE
FIRST_RIM = 76
FIRST_FACE = SHARE
RIM_WORDS = 13
AT_SPEED, AT_POPS, AT_NEXT, AT_MARKS, AT_Z, FACE_ROWS = 0, 12, 68, 88, 152, 160

f32 = jnp.float32
bf16 = jnp.bfloat16


def iota(shape, dim):
    return lax.broadcasted_iota(jnp.int32, shape, dim)


def roll(value, shift, axis):
    shift = shift % value.shape[axis]
    return pltpu.roll(value, shift, axis) if shift else value


def split_two(value):
    high = value.astype(bf16)
    return high, (value - high.astype(f32)).astype(bf16)


def call(kernel, out_shape, args, in_specs, scratch=()):
    vmem = pl.BlockSpec(memory_space=pltpu.VMEM)
    return pl.pallas_call(
        kernel,
        out_shape=out_shape,
        in_specs=in_specs,
        out_specs=[vmem] * len(out_shape),
        scratch_shapes=list(scratch),
        compiler_params=pltpu.CompilerParams(vmem_limit_bytes=32 * 1024 * 1024),
        interpret=INTERPRET,
    )(*args)


def moments_of(pops):
    density = pops[0]
    for member in range(1, 19):
        density = density + pops[member]
    parts = []
    for axis_no in range(3):
        total = None
        for member in range(19):
            if velocity_table[member][axis_no] == 1:
                total = pops[member] if total is None else total + pops[member]
        for member in range(19):
            if velocity_table[member][axis_no] == -1:
                total = total - pops[member]
        parts.append(total)
    inverse = 1.0 / density
    return density, [part * inverse for part in parts]


def relax_of(pops, density, speeds):
    factor = 18.0 * math.sqrt(2.0) * smag_const * smag_const
    moved = [density * part for part in speeds]
    pair = [pops[2 * k + 1] + pops[2 * k + 2] for k in range(9)]
    third = density * (1.0 / 3.0)
    xx = pair[0] + pair[3] + pair[4] + pair[5] + pair[6] - third - moved[0] * speeds[0]
    yy = pair[1] + pair[3] + pair[4] + pair[7] + pair[8] - third - moved[1] * speeds[1]
    zz = pair[2] + pair[5] + pair[6] + pair[7] + pair[8] - third - moved[2] * speeds[2]
    xy = pair[3] - pair[4] - moved[0] * speeds[1]
    xz = pair[5] - pair[6] - moved[0] * speeds[2]
    yz = pair[7] - pair[8] - moved[1] * speeds[2]
    norm_sq = xx * xx + yy * yy + zz * zz + 2.0 * (xy * xy + xz * xz + yz * yz)
    return 0.5 * (tau_base + jnp.sqrt(tau_base * tau_base + factor * jnp.sqrt(norm_sq) / density))


def along_of(member, speeds):
    total = None
    for axis_no in range(3):
        if velocity_table[member][axis_no] == 1:
            total = speeds[axis_no] if total is None else total + speeds[axis_no]
    for axis_no in range(3):
        if velocity_table[member][axis_no] == -1:
            total = total - speeds[axis_no]
    return total


def relaxed(pops, density, speeds, relax, pulls):
    pull = relax / density
    shifted = [speeds[a] + pull * pulls[a] for a in range(3)]
    shifted_sq = shifted[0] * shifted[0] + shifted[1] * shifted[1] + shifted[2] * shifted[2]
    rate = 1.0 / relax
    keep = 1.0 - rate
    scale = rate * density
    base = scale * (1.0 - 1.5 * shifted_sq)
    quad = 4.5 * scale
    results = [keep * pops[0] + base * (1.0 / 3.0)]
    for pair in range(9):
        plus = 2 * pair + 1
        along = along_of(plus, shifted)
        weight = 1.0 / 18.0 if pair < 3 else 1.0 / 36.0
        even = weight * (base + quad * along * along)
        odd = (3.0 * weight) * (scale * along)
        results.append(keep * pops[plus] + (even + odd))
        results.append(keep * pops[plus + 1] + (even - odd))
    return results


def along_x(mark, plane):
    base, frac = mark[0:1, :], mark[2:3, :]
    following = jnp.where(base == float(PLANES), 0.0, base)
    weight = jnp.where(base - 1.0 == plane, 1.0 - frac, 0.0)
    return jnp.where((base > 0.5) & (following == plane), frac, weight)


def block_weights(mark):
    base, frac = mark[1:2, :], mark[3:4, :]
    row = iota((ROWS, mark.shape[1]), 0).astype(f32)
    along_y = jnp.where(row == base, 1.0 - frac, jnp.where(row == base + 1.0, frac, 0.0))
    return [along_y * along_x(mark, float(plane)) for plane in range(PLANES)]


def spots(base_z):
    count = base_z.shape[1]
    return jnp.where(iota((LANES, count), 0).astype(f32) == base_z, 1.0, 0.0).astype(bf16)


def pairs_of(field):
    high, low = split_two(field)
    next_high, next_low = split_two(roll(field, -1, 1))
    return jnp.concatenate(
        [jnp.concatenate([high, low], 1), jnp.concatenate([next_high, next_low], 1)], 0
    )


def gathered(pairs, spot):
    return jnp.dot(pairs, jnp.concatenate([spot, spot], 0), preferred_element_type=f32)


def scattered(here, there, spot):
    size = here.shape[0]
    high, low = split_two(here)
    next_high, next_low = split_two(there)
    sums = lax.dot_general(
        jnp.concatenate([high, low, next_high, next_low], 0),
        spot,
        (((1,), (1,)), ((), ())),
        preferred_element_type=f32,
    )
    first = sums[0:size] + sums[size : 2 * size]
    second = sums[2 * size : 3 * size] + sums[3 * size :]
    return first + roll(second, 1, 1)


def forces_of(mark, weights, here, there):
    frac = mark[4:5, :]
    forces, spreads = [], []
    for axis_no in range(3):
        total = None
        for plane in range(PLANES):
            at = axis_no * PLANES + plane
            value = weights[plane] * (here[at] + frac * (there[at] - here[at]))
            total = value if total is None else total + value
        force = mark[5 + axis_no : 6 + axis_no, :] - jnp.sum(total, 0, keepdims=True)
        forces.append(force)
        for plane in range(PLANES):
            spreads.append(weights[plane] * force)
    return forces, spreads


def first_kernel(
    info_ref, count_ref, owner_hbm, cell_hbm, frac_hbm, speed_hbm, pops_hbm,
    send_ref, rank_ref, field_ref, density_ref, relax_ref,
    owner_ref, cell_ref, frac_ref, speed_ref, pops_ref, sems,
):
    copies = [
        pltpu.make_async_copy(source, target, sems.at[number])
        for number, (source, target) in enumerate(
            [
                (owner_hbm, owner_ref),
                (cell_hbm, cell_ref),
                (frac_hbm, frac_ref),
                (speed_hbm, speed_ref),
                (pops_hbm, pops_ref),
            ]
        )
    ]
    for copy in copies:
        copy.start()
    for copy in copies:
        copy.wait()
    owners, markers = send_ref.shape[0], owner_ref.shape[1]
    live = iota((1, markers), 1) < count_ref[0]
    owner = jnp.where(live, owner_ref[...], -1)
    base_z = cell_ref[2:3, :]
    upper, lower = base_z == LANES - 2, base_z == 0
    twin = jnp.where(
        upper,
        jnp.where(owner == owners - 1, 0, owner + 1),
        jnp.where(owner == 0, owners - 1, owner - 1),
    )
    twin = jnp.where(live & (upper | lower), twin, -1)
    hit = iota((owners, markers), 0) == owner
    hits = jnp.concatenate(
        [hit.astype(f32), (hit & upper).astype(f32), (hit & lower).astype(f32)], 0
    )
    below = (iota((LANES, LANES), 0) < iota((LANES, LANES), 1)).astype(bf16)
    before = jnp.zeros((3 * owners, 1), f32)
    ranks = [[], [], []]
    for start in range(0, markers, LANES):
        part = hits[:, start : start + LANES]
        inner = jnp.dot(part.astype(bf16), below, preferred_element_type=f32)
        picked = part * (inner + before)
        for kind in range(3):
            ranks[kind].append(
                jnp.sum(picked[kind * owners : (kind + 1) * owners], 0, keepdims=True)
            )
        before = before + jnp.sum(part, 1, keepdims=True)
    rank, rank_up, rank_low = [jnp.concatenate(kind, 1) for kind in ranks]
    rank_ref[...] = rank
    lane_up = jnp.where(rank_up < FEW, SLOTS + rank_up, FIRST_SPARE - FEW + rank_up)
    lane_low = jnp.where(
        rank_low < FEW, SLOTS + FEW + rank_low, FIRST_SPARE + SPARE - FEW + rank_low
    )
    lane_twin = jnp.where(upper, lane_up, lane_low)
    lane_z = FIRST_Z + jnp.where(rank >= 16.0, 2.0, jnp.where(rank >= 8.0, 1.0, 0.0))
    slot_z = rank - 8.0 * (lane_z - FIRST_Z)
    lane = iota((LANES, markers), 0).astype(f32)
    spot_own = (lane == rank).astype(bf16)
    spot_twin = (lane == lane_twin).astype(bf16)
    spot_z = (lane == lane_z).astype(bf16)
    row = iota((8, markers), 0)
    words = jnp.where(row == 0, cell_ref[0:1, :] + 1, cell_ref[1:2, :]).astype(f32)
    for number in range(3):
        words = jnp.where(row == 2 + number, frac_ref[number : number + 1, :], words)
        words = jnp.where(row == 5 + number, speed_ref[number : number + 1, :], words)
    high, low = split_two(words)
    high, low = high.astype(f32), low.astype(f32)
    words_z = jnp.where(row.astype(f32) == slot_z, base_z.astype(f32), 0.0)

    def to_owners(value, target):
        rows = [jnp.where(target == number, value, 0.0) for number in range(owners)]
        return jnp.concatenate(rows, 0).astype(bf16)

    def placed(left, spot):
        return lax.dot_general(left, spot, (((1,), (1,)), ((), ())), preferred_element_type=f32)

    tiles = placed(to_owners(high, owner), spot_own) + placed(to_owners(low, owner), spot_own)
    tiles = tiles + placed(to_owners(high, twin), spot_twin)
    tiles = tiles + placed(to_owners(low, twin), spot_twin)
    tiles = tiles + placed(to_owners(words_z, owner), spot_z)
    send_ref[...] = tiles.reshape(owners, 8, LANES)

    lane = iota((ROWS, LANES), 1)
    to_right, to_left = jnp.zeros((ROWS, LANES), f32), jnp.zeros((ROWS, LANES), f32)
    for plane in range(PLANES):
        pops = [pops_ref[member, plane] for member in range(19)]
        density, speeds = moments_of(pops)
        relax = relax_of(pops, density, speeds)
        density_ref[plane] = density
        relax_ref[plane] = relax
        for axis_no in range(3):
            at = axis_no * 32 + plane * 8
            field_ref[at : at + 8, :] = speeds[axis_no]
        common = [density, *speeds, relax]
        for word in range(RIM_WORDS):
            place = FIRST_RIM + word * PLANES + plane
            if word < 5:
                right, left, shift = common[word], common[word], 0
            elif word < 10:
                right, left, shift = pops[ahead_z[word - 5]], pops[back_z[word - 5]], 0
            else:
                right, left, shift = speeds[word - 10], speeds[word - 10], 1
            here = lane == place
            to_right = jnp.where(here, roll(right, place - (LANES - 1) + shift, 1), to_right)
            to_left = jnp.where(here, roll(left, place - shift, 1), to_left)
    left, right = info_ref[0], info_ref[1]
    send_ref[left] = send_ref[left] + to_left
    send_ref[right] = send_ref[right] + to_right


def second_kernel(
    info_ref, pops_ref, got_ref, field_ref, density_ref, relax_ref,
    next_ref, up_ref, down_ref,
    post_ref, near_ref, far_ref, left_ref, right_ref,
):
    left, right = info_ref[0], info_ref[1]
    lane = iota((ROWS, LANES), 1)
    row = iota((ROWS, LANES), 0)
    sources = got_ref.shape[0]

    chosen = iota((LANES, LANES), 1) % SHARE
    chosen = (iota((LANES, LANES), 0) == FIRST_Z + chosen // 8) & (chosen < SLOTS)
    every_z = jnp.dot(
        got_ref[...].reshape(sources * 8, LANES).astype(bf16),
        chosen.astype(bf16),
        preferred_element_type=f32,
    )
    marks, bases = [], []
    for tile in range(sources // 4):
        words, place = None, None
        for part in range(4):
            source = tile * 4 + part
            value = roll(got_ref[source], SHARE * part, 1)
            spot = every_z[source * 8 : source * 8 + 8, :]
            if part:
                words = jnp.where(lane // SHARE == part, value, words)
                place = jnp.where(lane // SHARE == part, spot, place)
            else:
                words, place = value, spot
        place = jnp.sum(jnp.where(lane % 8 == row, place, 0.0), 0, keepdims=True)
        place = jnp.where(iota((1, LANES), 1) % SHARE < SLOTS, place, -5.0)
        marks.append(words)
        bases.append(place)
        for ref in (up_ref, down_ref):
            ref[AT_MARKS + tile * 8 : AT_MARKS + tile * 8 + 8, :] = words
            ref[AT_Z + tile : AT_Z + tile + 1, :] = place

    ends = jnp.where(lane >= FIRST_RIM, got_ref[left], roll(got_ref[right], 64, 1))
    rim = [roll(ends, -(FIRST_RIM + PLANES * word), 1) for word in range(RIM_WORDS)]

    def spread_lane(value, at):
        return jnp.broadcast_to(value[:, at : at + 1], (ROWS, LANES))

    for axis_no in range(3):
        for plane in range(PLANES):
            at = axis_no * PLANES + plane
            near_ref[at] = spread_lane(rim[10 + axis_no], plane)
            near_ref[12 + at] = spread_lane(rim[1 + axis_no], 64 + plane)
            far_ref[at] = spread_lane(rim[1 + axis_no], plane)
            far_ref[12 + at] = spread_lane(rim[10 + axis_no], 64 + plane)
    left_ref[...] = jnp.zeros_like(left_ref)
    right_ref[...] = jnp.zeros_like(right_ref)

    def twins(mark, of_left, of_right):
        def both(ref):
            return [
                jnp.where(of_left, ref[at], jnp.where(of_right, ref[12 + at], 0.0))
                for at in range(12)
            ]

        return both(near_ref), both(far_ref)

    def keep_twins(mark, spreads, of_left, of_right):
        frac = mark[4:5, :]
        for at in range(12):
            ahead = spreads[at] * frac
            rows = slice(at * 8, at * 8 + 8)
            left_ref[rows, :] = left_ref[rows, :] + jnp.where(of_left, ahead, 0.0)
            right_ref[rows, :] = right_ref[rows, :] + jnp.where(of_right, spreads[at] - ahead, 0.0)

    of_left = (lane % SHARE >= SLOTS) & (lane % SHARE < SLOTS + FEW)
    of_right = lane % SHARE >= SLOTS + FEW
    near, far = twins(None, of_left, of_right)
    pairs = pairs_of(field_ref[...])
    force = jnp.zeros((96, LANES), f32)
    for block in range(sources // 8):
        mark = jnp.concatenate(marks[2 * block : 2 * block + 2], 1)
        spot = spots(jnp.concatenate(bases[2 * block : 2 * block + 2], 1))
        found = gathered(pairs, spot)
        weights = block_weights(mark)
        here = [found[at * 8 : at * 8 + 8] + jnp.concatenate([near[at]] * 2, 1) for at in range(12)]
        there = [
            found[96 + at * 8 : 104 + at * 8] + jnp.concatenate([far[at]] * 2, 1) for at in range(12)
        ]
        _, spreads = forces_of(mark, weights, here, there)
        for half in range(2):
            lanes = slice(half * LANES, (half + 1) * LANES)
            keep_twins(mark[:, lanes], [part[:, lanes] for part in spreads], of_left, of_right)
        spreads = jnp.concatenate(spreads, 0)
        ahead = spreads * mark[4:5, :]
        force = force + scattered(spreads - ahead, ahead, spot)

    further = jnp.where((lane >= FIRST_SPARE) & (lane < FIRST_Z), 1.0, 0.0)
    most = got_ref[0]
    for source in range(1, sources):
        most = jnp.maximum(most, got_ref[source])

    @pl.when(jnp.max(most * further) > 0.5)
    def _():
        lefts = lane < SPARE
        rights = (lane >= SPARE) & (lane < 2 * SPARE)
        near, far = twins(None, lefts, rights)

        def one(source, carry):
            mark = roll(got_ref[source], -FIRST_SPARE, 1)
            mark = jnp.where(lane < 2 * SPARE, mark, 0.0)
            _, spreads = forces_of(mark, block_weights(mark), near, far)
            keep_twins(mark, spreads, lefts, rights)
            return carry

        lax.fori_loop(0, sources, one, 0)

    left_high, left_low = split_two(left_ref[...])
    right_high, right_low = split_two(right_ref[...])
    column = iota((4 * LANES, LANES), 1) < 64
    whole = (iota((4 * LANES, LANES), 0) < 2 * LANES) == column
    sums = jnp.dot(
        jnp.concatenate([left_high, left_low, right_high, right_low], 1),
        jnp.where(whole, 1.0, 0.0).astype(bf16),
        preferred_element_type=f32,
    )
    pulls = []
    for axis_no in range(3):
        total = None
        for plane in range(PLANES):
            at = axis_no * 32 + plane * 8
            value = sums[at : at + 8, :]
            total = value if total is None else jnp.where(lane % PLANES == plane, value, total)
        pulls.append(total)
    density, speeds, relax = rim[0], rim[1:4], rim[4]
    pull = relax / density
    shifted = [speeds[a] + pull * pulls[a] for a in range(3)]
    shifted_sq = shifted[0] * shifted[0] + shifted[1] * shifted[1] + shifted[2] * shifted[2]
    rate = 1.0 / relax
    side = jnp.where(lane < 64, 1.0, -1.0)
    rim_post = []
    for number, member in enumerate(ahead_z):
        along = side * along_of(member, shifted)
        weight = 1.0 / 18.0 if number == 0 else 1.0 / 36.0
        target = weight * density * (1.0 + 3.0 * along + 4.5 * along * along - 1.5 * shifted_sq)
        rim_post.append((1.0 - rate) * rim[5 + number] + rate * target)

    for plane in range(PLANES):
        ats = [a * 32 + plane * 8 for a in range(3)]
        results = relaxed(
            [pops_ref[member, plane] for member in range(19)],
            density_ref[plane],
            [field_ref[at : at + 8, :] for at in ats],
            relax_ref[plane],
            [force[at : at + 8, :] for at in ats],
        )
        for member in range(19):
            post_ref[member, plane] = results[member]

    for plane in range(PLANES):
        pops = []
        for member in range(19):
            shift_x, shift_y, shift_z = velocity_table[member]
            source = (plane - shift_x) % PLANES
            value = post_ref[member, source]
            if shift_z == 1:
                edge = roll(rim_post[ahead_z.index(member)], -source, 1)
                value = jnp.where(lane == 0, edge, roll(value, 1, 1))
            if shift_z == -1:
                edge = roll(rim_post[back_z.index(member)], 63 - source, 1)
                value = jnp.where(lane == LANES - 1, edge, roll(value, -1, 1))
            if shift_y == 1:
                at = AT_NEXT + rising.index(member) * PLANES + plane
                up_ref[at : at + 1, :] = value[ROWS - 1 : ROWS, :]
                value = jnp.where(row == 0, post_ref[opposite[member], plane], roll(value, 1, 0))
            if shift_y == -1:
                at = AT_NEXT + falling.index(member) * PLANES + plane
                down_ref[at : at + 1, :] = value[0:1, :]
                value = jnp.where(
                    row == ROWS - 1, post_ref[opposite[member], plane], roll(value, -1, 0)
                )
            next_ref[member, plane] = value
            pops.append(value)
        _, speeds = moments_of(pops)
        for axis_no in range(3):
            at = AT_SPEED + axis_no * PLANES + plane
            up_ref[at : at + 1, :] = speeds[axis_no][ROWS - 2 : ROWS - 1, :]
            down_ref[at : at + 1, :] = speeds[axis_no][1:2, :]
        for number, member in enumerate(level + rising):
            at = AT_POPS + number * PLANES + plane
            up_ref[at : at + 1, :] = pops[member][ROWS - 1 : ROWS, :]
        for number, member in enumerate(level + falling):
            at = AT_POPS + number * PLANES + plane
            down_ref[at : at + 1, :] = pops[member][0:1, :]


def third_kernel(
    info_ref, next_ref, up_ref, down_ref, below_ref, above_ref,
    moved_ref, back_ref,
    wide_ref, field_ref, density_ref, post_ref, outer_ref,
):
    left, right, first_open, last_open, first_wall, last_wall = [info_ref[i] for i in range(6)]
    lane = iota((ROWS, LANES), 1)
    row = iota((ROWS, LANES), 0)
    sources = back_ref.shape[0]

    def four(ref, at):
        return ref[at : at + PLANES, :]

    for plane in range(PLANES):
        pops = []
        for member in range(19):
            value = next_ref[member, plane]
            if member in rising:
                at = AT_NEXT + rising.index(member) * PLANES + plane
                value = jnp.where(row == first_open, below_ref[at : at + 1, :], value)
            if member in falling:
                at = AT_NEXT + falling.index(member) * PLANES + plane
                value = jnp.where(row == last_open, above_ref[at : at + 1, :], value)
            wide_ref[member, plane] = value
            pops.append(value)
        density, speeds = moments_of(pops)
        density_ref[plane] = density
        for axis_no in range(3):
            at = axis_no * 32 + plane * 8
            field_ref[at : at + 8, :] = speeds[axis_no]

    outer = []
    for member in range(19):
        if member in falling:
            low = four(down_ref, AT_NEXT + falling.index(member) * PLANES)
        else:
            low = four(below_ref, AT_POPS + (level + rising).index(member) * PLANES)
        if member in rising:
            top = four(up_ref, AT_NEXT + rising.index(member) * PLANES)
        else:
            top = four(above_ref, AT_POPS + (level + falling).index(member) * PLANES)
        outer.append(jnp.concatenate([low, top], 0))
    outer_density, outer_speeds = moments_of(outer)
    lows, tops = [], []
    for axis_no in range(3):
        at = AT_SPEED + axis_no * PLANES
        second = jnp.concatenate([four(above_ref, at), four(below_ref, at)], 0)
        lows.append(jnp.where(row < PLANES, outer_speeds[axis_no], second))
        tops.append(jnp.where(row < PLANES, second, outer_speeds[axis_no]))

    def beyond(ref, field, base_y):
        pairs = pairs_of(jnp.concatenate(field, 0))
        total = jnp.zeros((24, LANES), f32)
        for block in range(sources // 8):
            tile = AT_MARKS + 16 * block
            mark = jnp.concatenate([ref[tile : tile + 8, :], ref[tile + 8 : tile + 16, :]], 1)
            at = AT_Z + 2 * block
            base = jnp.concatenate([ref[at : at + 1, :], ref[at + 1 : at + 2, :]], 1)
            spot = spots(base)
            found = gathered(pairs, spot)
            place = iota((ROWS, 2 * LANES), 0)
            frac = mark[3:4, :]
            weight = along_x(mark, (place % PLANES).astype(f32))
            weight = weight * jnp.where(place < PLANES, frac, 1.0 - frac)
            weight = jnp.where(mark[1:2, :] == base_y, weight, 0.0)
            frac = mark[4:5, :]
            spreads = []
            for axis_no in range(3):
                here = found[axis_no * 8 : axis_no * 8 + 8]
                there = found[24 + axis_no * 8 : 32 + axis_no * 8]
                value = weight * (here + frac * (there - here))
                force = mark[5 + axis_no : 6 + axis_no, :] - jnp.sum(value, 0, keepdims=True)
                spreads.append(weight * force)
            spreads = jnp.concatenate(spreads, 0)
            ahead = spreads * frac
            total = total + scattered(spreads - ahead, ahead, spot)
        return total

    from_below = beyond(below_ref, lows, float(ROWS - 2))
    from_above = beyond(above_ref, tops, 0.0)
    outer_pulls = [
        jnp.where(row < PLANES, from_below[a * 8 : a * 8 + 8], from_above[a * 8 : a * 8 + 8])
        for a in range(3)
    ]
    relax = relax_of(outer, outer_density, outer_speeds)
    outer_post = relaxed(outer, outer_density, outer_speeds, relax, outer_pulls)
    for number in range(5):
        outer_ref[number] = jnp.where(
            row < PLANES, outer_post[rising[number]], outer_post[falling[number]]
        )

    pairs = pairs_of(field_ref[...])
    total = jnp.zeros((96, LANES), f32)
    for block in range(sources // 8):
        tile = AT_MARKS + 16 * block
        mark = jnp.concatenate([up_ref[tile : tile + 8, :], up_ref[tile + 8 : tile + 16, :]], 1)
        at = AT_Z + 2 * block
        spot = spots(jnp.concatenate([up_ref[at : at + 1, :], up_ref[at + 1 : at + 2, :]], 1))
        found = gathered(pairs, spot)
        forces, spreads = forces_of(
            mark,
            block_weights(mark),
            [found[at * 8 : at * 8 + 8] for at in range(12)],
            [found[96 + at * 8 : 104 + at * 8] for at in range(12)],
        )
        spreads = jnp.concatenate(spreads, 0)
        ahead = spreads * mark[4:5, :]
        total = total + scattered(spreads - ahead, ahead, spot)
        for half in range(2):
            lanes = slice(half * LANES, (half + 1) * LANES)
            value = forces[2][:, lanes]
            value = jnp.where(row == 1, forces[1][:, lanes], value)
            value = jnp.where(row == 0, forces[0][:, lanes], value)
            for part in range(4):
                back_ref[block * 8 + half * 4 + part] = roll(value, -SHARE * part, 1)

    for plane in range(PLANES):
        ats = [a * 32 + plane * 8 for a in range(3)]
        pops = [wide_ref[member, plane] for member in range(19)]
        speeds = [field_ref[at : at + 8, :] for at in ats]
        density = density_ref[plane]
        relax = relax_of(pops, density, speeds)
        results = relaxed(pops, density, speeds, relax, [total[at : at + 8, :] for at in ats])
        for member in range(19):
            post_ref[member, plane] = results[member]

    to_right, to_left = jnp.zeros((ROWS, LANES), f32), jnp.zeros((ROWS, LANES), f32)
    for plane in range(PLANES):
        for member in range(19):
            shift_x, shift_y, shift_z = velocity_table[member]
            source = (plane - shift_x) % PLANES
            value = post_ref[member, source]
            if shift_y == 1:
                edge = outer_ref[rising.index(member), source : source + 1, :]
                value = jnp.where(row == 0, edge, roll(value, 1, 0))
            if shift_y == -1:
                at = PLANES + source
                edge = outer_ref[falling.index(member), at : at + 1, :]
                value = jnp.where(row == ROWS - 1, edge, roll(value, -1, 0))
            if shift_z:
                value = roll(value, shift_z, 1)
            if shift_z == 1:
                place = FIRST_FACE + ahead_z.index(member) * PLANES + plane
                to_right = jnp.where(lane == place, roll(value, place, 1), to_right)
            if shift_z == -1:
                place = FIRST_FACE + back_z.index(member) * PLANES + plane
                to_left = jnp.where(lane == place, roll(value, place + 1, 1), to_left)
            if shift_y == 1:
                value = jnp.where(row == first_wall, post_ref[opposite[member], plane], value)
            if shift_y == -1:
                value = jnp.where(row == last_wall, post_ref[opposite[member], plane], value)
            moved_ref[member, plane] = value
    faces = (lane >= FIRST_FACE) & (lane < FIRST_FACE + 5 * PLANES)
    back_ref[left] = jnp.where(faces, to_left, back_ref[left])
    back_ref[right] = jnp.where(faces, to_right, back_ref[right])


def last_kernel(info_ref, count_ref, moved_ref, got_ref, owner_ref, rank_ref, pops_ref, force_ref):
    left, right, _, _, first_wall, last_wall = [info_ref[i] for i in range(6)]
    lane = iota((ROWS, LANES), 1)
    row = iota((ROWS, LANES), 0)
    from_left, from_right = got_ref[left], got_ref[right]
    for member in range(19):
        _, shift_y, shift_z = velocity_table[member]
        for plane in range(PLANES):
            value = moved_ref[member, plane]
            if shift_z:
                if shift_z == 1:
                    place = FIRST_FACE + ahead_z.index(member) * PLANES + plane
                    edge, here = roll(from_left, -place, 1), lane == 0
                else:
                    place = FIRST_FACE + back_z.index(member) * PLANES + plane
                    edge, here = roll(from_right, LANES - 1 - place, 1), lane == LANES - 1
                if shift_y == 1:
                    here = here & (row != first_wall)
                if shift_y == -1:
                    here = here & (row != last_wall)
                value = jnp.where(here, edge, value)
            pops_ref[member, plane] = value
    owners, markers = got_ref.shape[0], owner_ref.shape[1]
    live = iota((1, markers), 1) < count_ref[0]
    owner = jnp.where(live, owner_ref[...], -1)
    spot = (iota((LANES, markers), 0).astype(f32) == rank_ref[...]).astype(bf16)
    high, low = split_two(got_ref[...].reshape(owners * 8, LANES))
    found = jnp.dot(
        jnp.concatenate([high, low], 1),
        jnp.concatenate([spot, spot], 0),
        preferred_element_type=f32,
    )
    total = jnp.zeros((8, markers), f32)
    for number in range(owners):
        total = jnp.where(owner == number, found[number * 8 : number * 8 + 8, :], total)
    force_ref[...] = total[0:3, :] / ref_speed


def body(populations, marker_owner, marker_cell, marker_frac, marker_speed, marker_count):
    count_gy, count_gz = lax.axis_size("gy"), lax.axis_size("gz")
    markers = marker_owner.shape[0]
    smem = pl.BlockSpec(memory_space=pltpu.SMEM)
    vmem = pl.BlockSpec(memory_space=pltpu.VMEM)
    hbm = pl.BlockSpec(memory_space=pl.ANY)
    shape = jax.ShapeDtypeStruct
    row, column = lax.axis_index("gy"), lax.axis_index("gz")
    first, last = row == 0, row == count_gy - 1
    info = jnp.stack(
        [
            (column + count_gz - 1) % count_gz,
            (column + 1) % count_gz,
            jnp.where(first, -1, 0),
            jnp.where(last, -1, ROWS - 1),
            jnp.where(first, 0, -1),
            jnp.where(last, ROWS - 1, -1),
        ]
    ).astype(jnp.int32)
    owner = marker_owner.reshape(1, markers)
    tiles = shape((count_gz, 8, LANES), f32)
    field = shape((96, LANES), f32)
    cells = shape((PLANES, ROWS, LANES), f32)
    lattice = shape(populations.shape, f32)
    send, rank, speeds, density, relax = call(
        first_kernel,
        [tiles, shape((1, markers), f32), field, cells, cells],
        [info, marker_count, owner, marker_cell, marker_frac, marker_speed, populations],
        [smem] * 2 + [hbm] * 5,
        scratch=[
            pltpu.VMEM((1, markers), jnp.int32),
            pltpu.VMEM((3, markers), jnp.int32),
            pltpu.VMEM((3, markers), f32),
            pltpu.VMEM((3, markers), f32),
            pltpu.VMEM(populations.shape, f32),
            pltpu.SemaphoreType.DMA((5,)),
        ],
    )
    got = lax.all_to_all(send, "gz", split_axis=0, concat_axis=0, tiled=True)
    face = shape((FACE_ROWS, LANES), f32)
    next_pops, up, down = call(
        second_kernel,
        [lattice, face, face],
        [info, populations, got, speeds, density, relax],
        [smem] + [vmem] * 5,
        scratch=[
            pltpu.VMEM(populations.shape, f32),
            pltpu.VMEM((24, ROWS, LANES), f32),
            pltpu.VMEM((24, ROWS, LANES), f32),
            pltpu.VMEM((96, LANES), f32),
            pltpu.VMEM((96, LANES), f32),
        ],
    )
    below = lax.ppermute(up, "gy", [(i, (i + 1) % count_gy) for i in range(count_gy)])
    above = lax.ppermute(down, "gy", [((i + 1) % count_gy, i) for i in range(count_gy)])
    moved, back = call(
        third_kernel,
        [lattice, tiles],
        [info, next_pops, up, down, below, above],
        [smem] + [vmem] * 5,
        scratch=[
            pltpu.VMEM(populations.shape, f32),
            pltpu.VMEM((96, LANES), f32),
            pltpu.VMEM((PLANES, ROWS, LANES), f32),
            pltpu.VMEM(populations.shape, f32),
            pltpu.VMEM((5, ROWS, LANES), f32),
        ],
    )
    back = lax.all_to_all(back, "gz", split_axis=0, concat_axis=0, tiled=True)
    pops, force = call(
        last_kernel,
        [lattice, shape((3, markers), f32)],
        [info, marker_count, moved, back, owner, rank],
        [smem] * 2 + [vmem] * 4,
    )
    return pops, force


def solution(mesh):
    return jax.shard_map(
        body,
        mesh=mesh,
        in_specs=(
            P(None, None, "gy", "gz"),
            P(("gy", "gz"), None),
            P(None, ("gy", "gz")),
            P(None, ("gy", "gz")),
            P(None, ("gy", "gz")),
            P(("gy", "gz")),
        ),
        out_specs=(P(None, None, "gy", "gz"), P(None, ("gy", "gz"))),
        check_vma=False,
    )
```

profile of v0, /device:TPU:1, one launch (start us, length us, event | category | flops | bytes accessed | tf_op | source)
XLA Modules:
  0.0 68.5 jit_solution(2045881152435546212)
XLA Ops:
  0.7 0.0 copy-start.5
  1.3 0.0 copy-start.4
  1.3 0.0 copy-start.3
  1.4 0.0 copy-start.2
  1.4 0.1 stack.27.info_ref
  1.4 0.0 copy-done.5
  1.5 0.6 copy-done.4
  2.0 0.0 copy-done.3
  2.0 0.0 copy-done.2
  2.0 0.0 copy-start
  2.1 1.0 %copy-done = f32[19,4,8,128]{3,2,1,0:T(8,128)S(1)} copy-done((f32[19,4,8,128]{3,2,1,0:T(8,128)S(1)}, f32[19,4,8,128]{3,2,1,0:T(8,128)}, u32[]{:S(2)}) %copy-start) | copy-done | bytes 311320
  3.0 0.0 copy-start.1
  3.0 1.5 %shard_map.77 = (f32[32,8,128]{2,1,0:T(8,128)S(1)}, f32[1,512]{1,0:T(1,128)S(1)}, f32[96,128]{1,0:T(8,128)S(1)}, f32[4,8,128]{2,1,0:T(8,128)S(1)}, f32[4,8,128]{2,1,0:T(8,128)S(1)}) custom-call(s32[6]{0:T(128)S(1)} %stack.27.info_ref, s32[1]{0:T(128)S(6)} %copy.8.count_ref, s32[1,512]{1,0:T(1,128)S(1)} %bitcast.7, s32[3,512]{1,0:T(4,128)S(1)} %copy-done.3, ...), custom_call_target="tpu_custom_call" | custom-call | tf_op jit(solution)/shard_map/pallas_call | solution.py:77
  4.5 27.6 %all_to_all.10.got_ref = f32[32,8,128]{2,1,0:T(8,128)S(1)} all-to-all(f32[32,8,128]{2,1,0:T(8,128)S(1)} %get-tuple-element.12), channel_id=1, replica_groups=mesh['gy'=32,'gz'=32] {'gz'}, dimensions={0} | all-to-all | bytes 262144 | tf_op jit(solution)/shard_map/all_to_all | solution.py:750
  32.1 0.0 copy-done.1
  32.1 1.8 %shard_map.78 = (f32[19,4,8,128]{3,2,1,0:T(8,128)S(1)}, f32[160,128]{1,0:T(8,128)S(1)}, f32[160,128]{1,0:T(8,128)S(1)}) custom-call(s32[6]{0:T(128)S(1)} %stack.27.info_ref, f32[19,4,8,128]{3,2,1,0:T(8,128)S(1)} %copy-done.1, f32[32,8,128]{2,1,0:T(8,128)S(1)} %all_to_all.10.got_ref, f32[96,128]{1,0:T(8,128)S(1)} %get-tuple-element.13.field_ref, ...), custom_call_target="tpu_custom_call" | custom-call | tf_op jit(solution)/shard_map/pallas_call | solution.py:77
  33.9 1.9 %collective-permute-start = (f32[160,128]{1,0:T(8,128)S(1)}, f32[160,128]{1,0:T(8,128)S(1)}, u32[]{:S(2)}, u32[]{:S(2)}) collective-permute-start(f32[160,128]{1,0:T(8,128)S(1)} %get-tuple-element.17.up_ref), channel_id=1, source_target_pairs={{0,32},{32,64},{64,96},{96,128},{128,160},{160,192},{192,224},{224... | collective-permute-start | bytes 245768 | tf_op jit(solution)/shard_map/ppermute | solution.py:765
  35.8 12.7 %collective-permute-start.1 = (f32[160,128]{1,0:T(8,128)S(1)}, f32[160,128]{1,0:T(8,128)S(1)}, u32[]{:S(2)}, u32[]{:S(2)}) collective-permute-start(f32[160,128]{1,0:T(8,128)S(1)} %get-tuple-element.18.down_ref), channel_id=1, source_target_pairs={{32,0},{64,32},{96,64},{128,96},{160,128},{192,160},{224,192},{256... | collective-permute-start | bytes 245768 | tf_op jit(solution)/shard_map/ppermute | solution.py:766
  48.5 0.7 %collective-permute-done.below_ref = f32[160,128]{1,0:T(8,128)S(1)} collective-permute-done((f32[160,128]{1,0:T(8,128)S(1)}, f32[160,128]{1,0:T(8,128)S(1)}, u32[]{:S(2)}, u32[]{:S(2)}) %collective-permute-start) | collective-permute-done | bytes 81952 | tf_op jit(solution)/shard_map/ppermute | solution.py:765
  49.2 0.7 %collective-permute-done.1.above_ref = f32[160,128]{1,0:T(8,128)S(1)} collective-permute-done((f32[160,128]{1,0:T(8,128)S(1)}, f32[160,128]{1,0:T(8,128)S(1)}, u32[]{:S(2)}, u32[]{:S(2)}) %collective-permute-start.1) | collective-permute-done | bytes 81952 | tf_op jit(solution)/shard_map/ppermute | solution.py:766
  49.9 2.1 %shard_map.79 = (f32[19,4,8,128]{3,2,1,0:T(8,128)S(1)}, f32[32,8,128]{2,1,0:T(8,128)S(1)}) custom-call(s32[6]{0:T(128)S(1)} %stack.27.info_ref, f32[19,4,8,128]{3,2,1,0:T(8,128)S(1)} %get-tuple-element.16.next_ref, f32[160,128]{1,0:T(8,128)S(1)} %get-tuple-element.17.up_ref, f32[160,128]{1,0:T(8,128)S(1)} %get-tuple-element.18.down_ref, ...), custom_call_target="tpu_custom_call" | custom-call | tf_op jit(solution)/shard_map/pallas_call | solution.py:77
  52.1 15.0 %all_to_all.11.got_ref = f32[32,8,128]{2,1,0:T(8,128)S(1)} all-to-all(f32[32,8,128]{2,1,0:T(8,128)S(1)} %get-tuple-element.20), channel_id=1, replica_groups=mesh['gy'=32,'gz'=32] {'gz'}, dimensions={0} | all-to-all | bytes 262144 | tf_op jit(solution)/shard_map/all_to_all | solution.py:780
  67.1 1.4 %shard_map.80 = (f32[19,4,8,128]{3,2,1,0:T(8,128)}, f32[3,512]{1,0:T(4,128)}) custom-call(s32[6]{0:T(128)S(1)} %stack.27.info_ref, s32[1]{0:T(128)S(6)} %copy.8.count_ref, f32[19,4,8,128]{3,2,1,0:T(8,128)S(1)} %get-tuple-element.19.moved_ref, f32[32,8,128]{2,1,0:T(8,128)S(1)} %all_to_all.11.got_ref, s32[1,512]{1,0:T(1,128)S(1)} %bitcast.8, ...), custom_call_target="tpu_custom_call" | custom-call | tf_op jit(solution)/shard_map/pallas_call | solution.py:77
Async XLA Ops:
  0.7 0.8 %copy-start.5 = (f32[3,512]{1,0:T(4,128)S(1)}, f32[3,512]{1,0:T(4,128)}, u32[]{:S(2)}) copy-start(f32[3,512]{1,0:T(4,128)} %speed_hbm.1) | copy-start | bytes 18436
  1.3 0.7 %copy-start.4 = (f32[3,512]{1,0:T(4,128)S(1)}, f32[3,512]{1,0:T(4,128)}, u32[]{:S(2)}) copy-start(f32[3,512]{1,0:T(4,128)} %frac_hbm.1) | copy-start | bytes 18436
  1.3 0.7 %copy-start.3 = (s32[3,512]{1,0:T(4,128)S(1)}, s32[3,512]{1,0:T(4,128)}, u32[]{:S(2)}) copy-start(s32[3,512]{1,0:T(4,128)} %cell_hbm.1) | copy-start | bytes 18436
  1.4 0.7 %copy-start.2 = (s32[512,1]{0,1:T(1,128)S(1)}, s32[512,1]{0,1:T(1,128)}, u32[]{:S(2)}) copy-start(s32[512,1]{0,1:T(1,128)} %param.7) | copy-start | bytes 6148
  2.0 1.0 %copy-start = (f32[19,4,8,128]{3,2,1,0:T(8,128)S(1)}, f32[19,4,8,128]{3,2,1,0:T(8,128)}, u32[]{:S(2)}) copy-start(f32[19,4,8,128]{3,2,1,0:T(8,128)} %pops_ref.1) | copy-start | bytes 933892
  3.0 29.1 %copy-start.1 = (f32[19,4,8,128]{3,2,1,0:T(8,128)S(1)}, f32[19,4,8,128]{3,2,1,0:T(8,128)}, u32[]{:S(2)}) copy-start(f32[19,4,8,128]{3,2,1,0:T(8,128)} %pops_ref.1) | copy-start | bytes 933892
  33.9 15.4 %collective-permute-start = (f32[160,128]{1,0:T(8,128)S(1)}, f32[160,128]{1,0:T(8,128)S(1)}, u32[]{:S(2)}, u32[]{:S(2)}) collective-permute-start(f32[160,128]{1,0:T(8,128)S(1)} %get-tuple-element.17.up_ref), channel_id=1, source_target_pairs={{0,32},{32,64},{64,96},{96,128},{128,160},{160,192},{192,224},{224... | collective-permute-start | bytes 245768 | tf_op jit(solution)/shard_map/ppermute | solution.py:765
  35.8 14.2 %collective-permute-start.1 = (f32[160,128]{1,0:T(8,128)S(1)}, f32[160,128]{1,0:T(8,128)S(1)}, u32[]{:S(2)}, u32[]{:S(2)}) collective-permute-start(f32[160,128]{1,0:T(8,128)S(1)} %get-tuple-element.18.down_ref), channel_id=1, source_target_pairs={{32,0},{64,32},{96,64},{128,96},{160,128},{192,160},{224,192},{256... | collective-permute-start | bytes 245768 | tf_op jit(solution)/shard_map/ppermute | solution.py:766
where the time goes:
time: 68.9 us; the launch traced here: 68.5 us
  blocking collectives  42.6 us (62%)
  starting transfers between devices  14.6 us (21%)
  Pallas kernels  6.81 us (10%)
  local copies, waits for them, and re-layouts  1.66 us (2%)
  waiting for transfers between devices  1.46 us (2%)
  between operations  1.4 us (2%)
    all_to_all x1, blocking collectives, body(): got = lax.all_to_all(send, 'gz', split_axis=0, concat_axis=0, tiled=True)  27.6 us
    all_to_all x1, blocking collectives, body(): back = lax.all_to_all(back, 'gz', split_axis=0, concat_axis=0, tiled=True)  15 us
    ppermute x1, starting transfers between devices, body(): lax.ppermute(down, 'gy', [((i + 1) % count_gy, i) for i in range(count_gy)])  12.7 us
    pallas_call x4, Pallas kernels, call(): pl.pallas_call(kernel, out_shape=out_shape, in_specs=in_specs, out_specs=...  6.81 us
    ppermute x1, starting transfers between devices, body(): lax.ppermute(up, 'gy', [(i, (i + 1) % count_gy) for i in range(count_gy)])  1.92 us
    unnamed x12, local copies, waits for them, and re-layouts  1.58 us
  transfers between devices with their start and end apart: 2, of which 2 were waited for; matrix products, arithmetic and copies ran while one was open for 0% of the time, Pallas kernels for 0%

commit v1 on v0

--- a/solution.py
+++ b/solution.py
@@ -50,7 +50,8 @@
 FIRST_SPARE = SHARE
 FIRST_Z = SHARE + 2 * SPARE
 FIRST_RIM = 76
-FIRST_FACE = SHARE
+LATE_FACE = 3 * SHARE
+EARLY = 16
 RIM_WORDS = 13
 AT_SPEED, AT_POPS, AT_NEXT, AT_MARKS, AT_Z, FACE_ROWS = 0, 12, 68, 88, 152, 160
 
@@ -181,7 +182,7 @@
     return jnp.dot(pairs, jnp.concatenate([spot, spot], 0), preferred_element_type=f32)
 
 
-def scattered(here, there, spot):
+def sums_of(here, there, spot):
     size = here.shape[0]
     high, low = split_two(here)
     next_high, next_low = split_two(there)
@@ -193,6 +194,11 @@
     )
     first = sums[0:size] + sums[size : 2 * size]
     second = sums[2 * size : 3 * size] + sums[3 * size :]
+    return first, second
+
+
+def scattered(here, there, spot):
+    first, second = sums_of(here, there, spot)
     return first + roll(second, 1, 1)
 
 
@@ -231,7 +237,7 @@
     ]
     for copy in copies:
         copy.start()
-    for copy in copies:
+    for copy in copies[0:4]:
         copy.wait()
     owners, markers = send_ref.shape[0], owner_ref.shape[1]
     live = iota((1, markers), 1) < count_ref[0]
@@ -295,6 +301,7 @@
     tiles = tiles + placed(to_owners(words_z, owner), spot_z)
     send_ref[...] = tiles.reshape(owners, 8, LANES)
 
+    copies[4].wait()
     lane = iota((ROWS, LANES), 1)
     to_right, to_left = jnp.zeros((ROWS, LANES), f32), jnp.zeros((ROWS, LANES), f32)
     for plane in range(PLANES):
@@ -326,7 +333,7 @@
 def second_kernel(
     info_ref, pops_ref, got_ref, field_ref, density_ref, relax_ref,
     next_ref, up_ref, down_ref,
-    post_ref, near_ref, far_ref, left_ref, right_ref,
+    post_ref, near_ref, far_ref, twin_ref,
 ):
     left, right = info_ref[0], info_ref[1]
     lane = iota((ROWS, LANES), 1)
@@ -373,10 +380,8 @@
             near_ref[12 + at] = spread_lane(rim[1 + axis_no], 64 + plane)
             far_ref[at] = spread_lane(rim[1 + axis_no], plane)
             far_ref[12 + at] = spread_lane(rim[10 + axis_no], 64 + plane)
-    left_ref[...] = jnp.zeros_like(left_ref)
-    right_ref[...] = jnp.zeros_like(right_ref)
-
-    def twins(mark, of_left, of_right):
+
+    def twins(of_left, of_right):
         def both(ref):
             return [
                 jnp.where(of_left, ref[at], jnp.where(of_right, ref[12 + at], 0.0))
@@ -385,17 +390,21 @@
 
         return both(near_ref), both(far_ref)
 
-    def keep_twins(mark, spreads, of_left, of_right):
-        frac = mark[4:5, :]
-        for at in range(12):
-            ahead = spreads[at] * frac
-            rows = slice(at * 8, at * 8 + 8)
-            left_ref[rows, :] = left_ref[rows, :] + jnp.where(of_left, ahead, 0.0)
-            right_ref[rows, :] = right_ref[rows, :] + jnp.where(of_right, spreads[at] - ahead, 0.0)
+    def sides(lefts, rights, count):
+        place, member = iota((LANES, count), 0), iota((LANES, count), 1)
+        chosen = jnp.where(place < 64, lefts(member).astype(f32), rights(member).astype(f32))
+        return chosen.astype(bf16)
 
     of_left = (lane % SHARE >= SLOTS) & (lane % SHARE < SLOTS + FEW)
     of_right = lane % SHARE >= SLOTS + FEW
-    near, far = twins(None, of_left, of_right)
+    near, far = twins(of_left, of_right)
+    side = sides(
+        lambda member: (member % SHARE >= SLOTS) & (member % SHARE < SLOTS + FEW),
+        lambda member: member % SHARE >= SLOTS + FEW,
+        2 * LANES,
+    )
+    of_rim = jnp.zeros((96, LANES), f32)
+    rim_left = iota((96, LANES), 1) < 64
     pairs = pairs_of(field_ref[...])
     force = jnp.zeros((96, LANES), f32)
     for block in range(sources // 8):
@@ -408,12 +417,12 @@
             found[96 + at * 8 : 104 + at * 8] + jnp.concatenate([far[at]] * 2, 1) for at in range(12)
         ]
         _, spreads = forces_of(mark, weights, here, there)
-        for half in range(2):
-            lanes = slice(half * LANES, (half + 1) * LANES)
-            keep_twins(mark[:, lanes], [part[:, lanes] for part in spreads], of_left, of_right)
         spreads = jnp.concatenate(spreads, 0)
         ahead = spreads * mark[4:5, :]
-        force = force + scattered(spreads - ahead, ahead, spot)
+        first, second = sums_of(spreads - ahead, ahead, jnp.concatenate([spot, side], 0))
+        force = force + (first[:, 0:LANES] + roll(second[:, 0:LANES], 1, 1))
+        of_rim = of_rim + jnp.where(rim_left, second[:, LANES:], first[:, LANES:])
+    twin_ref[...] = of_rim
 
     further = jnp.where((lane >= FIRST_SPARE) & (lane < FIRST_Z), 1.0, 0.0)
     most = got_ref[0]
@@ -422,28 +431,22 @@
 
     @pl.when(jnp.max(most * further) > 0.5)
     def _():
-        lefts = lane < SPARE
-        rights = (lane >= SPARE) & (lane < 2 * SPARE)
-        near, far = twins(None, lefts, rights)
+        near, far = twins(lane < SPARE, lane >= SPARE)
+        side = sides(lambda member: member < SPARE, lambda member: member >= SPARE, LANES)
 
         def one(source, carry):
             mark = roll(got_ref[source], -FIRST_SPARE, 1)
             mark = jnp.where(lane < 2 * SPARE, mark, 0.0)
             _, spreads = forces_of(mark, block_weights(mark), near, far)
-            keep_twins(mark, spreads, lefts, rights)
+            spreads = jnp.concatenate(spreads, 0)
+            ahead = spreads * mark[4:5, :]
+            first, second = sums_of(spreads - ahead, ahead, side)
+            twin_ref[...] = twin_ref[...] + jnp.where(rim_left, second, first)
             return carry
 
         lax.fori_loop(0, sources, one, 0)
 
-    left_high, left_low = split_two(left_ref[...])
-    right_high, right_low = split_two(right_ref[...])
-    column = iota((4 * LANES, LANES), 1) < 64
-    whole = (iota((4 * LANES, LANES), 0) < 2 * LANES) == column
-    sums = jnp.dot(
-        jnp.concatenate([left_high, left_low, right_high, right_low], 1),
-        jnp.where(whole, 1.0, 0.0).astype(bf16),
-        preferred_element_type=f32,
-    )
+    sums = twin_ref[...]
     pulls = []
     for axis_no in range(3):
         total = None
@@ -457,10 +460,10 @@
     shifted = [speeds[a] + pull * pulls[a] for a in range(3)]
     shifted_sq = shifted[0] * shifted[0] + shifted[1] * shifted[1] + shifted[2] * shifted[2]
     rate = 1.0 / relax
-    side = jnp.where(lane < 64, 1.0, -1.0)
+    sign = jnp.where(lane < 64, 1.0, -1.0)
     rim_post = []
     for number, member in enumerate(ahead_z):
-        along = side * along_of(member, shifted)
+        along = sign * along_of(member, shifted)
         weight = 1.0 / 18.0 if number == 0 else 1.0 / 36.0
         target = weight * density * (1.0 + 3.0 * along + 4.5 * along * along - 1.5 * shifted_sq)
         rim_post.append((1.0 - rate) * rim[5 + number] + rate * target)
@@ -607,6 +610,7 @@
 
     pairs = pairs_of(field_ref[...])
     total = jnp.zeros((96, LANES), f32)
+    kept = [jnp.zeros((ROWS, LANES), f32) for axis_no in range(3)]
     for block in range(sources // 8):
         tile = AT_MARKS + 16 * block
         mark = jnp.concatenate([up_ref[tile : tile + 8, :], up_ref[tile + 8 : tile + 16, :]], 1)
@@ -624,11 +628,18 @@
         total = total + scattered(spreads - ahead, ahead, spot)
         for half in range(2):
             lanes = slice(half * LANES, (half + 1) * LANES)
-            value = forces[2][:, lanes]
-            value = jnp.where(row == 1, forces[1][:, lanes], value)
-            value = jnp.where(row == 0, forces[0][:, lanes], value)
-            for part in range(4):
-                back_ref[block * 8 + half * 4 + part] = roll(value, -SHARE * part, 1)
+            for axis_no in range(3):
+                kept[axis_no] = jnp.where(
+                    row == 2 * block + half, forces[axis_no][:, lanes], kept[axis_no]
+                )
+    back_ref[...] = jnp.zeros(back_ref.shape, f32)
+    for part in range(4):
+        value = roll(kept[0], -SHARE * part, 1)
+        for axis_no in range(1, 3):
+            moved = roll(kept[axis_no], SHARE * (axis_no - part), 1)
+            value = jnp.where(lane // SHARE == axis_no, moved, value)
+        for tile in range(sources // 4):
+            back_ref[4 * tile + part, 0:1, :] = value[tile : tile + 1, :]
 
     for plane in range(PLANES):
         ats = [a * 32 + plane * 8 for a in range(3)]
@@ -656,36 +667,55 @@
             if shift_z:
                 value = roll(value, shift_z, 1)
             if shift_z == 1:
-                place = FIRST_FACE + ahead_z.index(member) * PLANES + plane
+                place = ahead_z.index(member) * PLANES + plane
                 to_right = jnp.where(lane == place, roll(value, place, 1), to_right)
             if shift_z == -1:
-                place = FIRST_FACE + back_z.index(member) * PLANES + plane
+                place = back_z.index(member) * PLANES + plane
                 to_left = jnp.where(lane == place, roll(value, place + 1, 1), to_left)
             if shift_y == 1:
                 value = jnp.where(row == first_wall, post_ref[opposite[member], plane], value)
             if shift_y == -1:
                 value = jnp.where(row == last_wall, post_ref[opposite[member], plane], value)
             moved_ref[member, plane] = value
-    faces = (lane >= FIRST_FACE) & (lane < FIRST_FACE + 5 * PLANES)
-    back_ref[left] = jnp.where(faces, to_left, back_ref[left])
-    back_ref[right] = jnp.where(faces, to_right, back_ref[right])
+    for target, face in ((left, to_left), (right, to_right)):
+        early, late = jnp.zeros((ROWS, LANES), f32), jnp.zeros((ROWS, LANES), f32)
+        for number in range(ROWS):
+            early = jnp.where(row == number, roll(face, EARLY * number, 1), early)
+            late = jnp.where(row == number, roll(face, LATE_FACE - EARLY + 4 * number, 1), late)
+        early = jnp.where(lane // EARLY == row, early, 0.0)
+        late = jnp.where((lane - LATE_FACE) // 4 == row, late, 0.0)
+        late = jnp.where(lane >= LATE_FACE, late, 0.0)
+        mine = jnp.where(iota((1, LANES), 1) < LATE_FACE, back_ref[target, 0:1, :], 0.0)
+        back_ref[target, 0:1, :] = mine + jnp.sum(late, 0, keepdims=True)
+        back_ref[target, 1:2, :] = jnp.sum(early, 0, keepdims=True)
 
 
 def last_kernel(info_ref, count_ref, moved_ref, got_ref, owner_ref, rank_ref, pops_ref, force_ref):
     left, right, _, _, first_wall, last_wall = [info_ref[i] for i in range(6)]
     lane = iota((ROWS, LANES), 1)
     row = iota((ROWS, LANES), 0)
-    from_left, from_right = got_ref[left], got_ref[right]
+
+    def face_of(source):
+        late = jnp.broadcast_to(got_ref[source, 0:1, :], (ROWS, LANES))
+        early = jnp.broadcast_to(got_ref[source, 1:2, :], (ROWS, LANES))
+        face = jnp.zeros((ROWS, LANES), f32)
+        for number in range(ROWS):
+            value = roll(late, EARLY - LATE_FACE - 4 * number, 1)
+            value = jnp.where(lane < EARLY, roll(early, -EARLY * number, 1), value)
+            face = jnp.where(row == number, value, face)
+        return face
+
+    from_left, from_right = face_of(left), face_of(right)
     for member in range(19):
         _, shift_y, shift_z = velocity_table[member]
         for plane in range(PLANES):
             value = moved_ref[member, plane]
             if shift_z:
                 if shift_z == 1:
-                    place = FIRST_FACE + ahead_z.index(member) * PLANES + plane
+                    place = ahead_z.index(member) * PLANES + plane
                     edge, here = roll(from_left, -place, 1), lane == 0
                 else:
-                    place = FIRST_FACE + back_z.index(member) * PLANES + plane
+                    place = back_z.index(member) * PLANES + plane
                     edge, here = roll(from_right, LANES - 1 - place, 1), lane == LANES - 1
                 if shift_y == 1:
                     here = here & (row != first_wall)
@@ -697,16 +727,19 @@
     live = iota((1, markers), 1) < count_ref[0]
     owner = jnp.where(live, owner_ref[...], -1)
     spot = (iota((LANES, markers), 0).astype(f32) == rank_ref[...]).astype(bf16)
-    high, low = split_two(got_ref[...].reshape(owners * 8, LANES))
+    rows = got_ref[:, 0, :]
+    high, low = split_two(
+        jnp.concatenate([roll(rows, -SHARE * axis_no, 1) for axis_no in range(3)], 0)
+    )
     found = jnp.dot(
         jnp.concatenate([high, low], 1),
         jnp.concatenate([spot, spot], 0),
         preferred_element_type=f32,
     )
-    total = jnp.zeros((8, markers), f32)
-    for number in range(owners):
-        total = jnp.where(owner == number, found[number * 8 : number * 8 + 8, :], total)
-    force_ref[...] = total[0:3, :] / ref_speed
+    hit = iota((owners, markers), 0) == owner
+    for axis_no in range(3):
+        value = jnp.where(hit, found[axis_no * owners : (axis_no + 1) * owners], 0.0)
+        force_ref[axis_no : axis_no + 1, :] = jnp.sum(value, 0, keepdims=True) / ref_speed
 
 
 def body(populations, marker_owner, marker_cell, marker_frac, marker_speed, marker_count):
@@ -714,7 +747,7 @@
     markers = marker_owner.shape[0]
     smem = pl.BlockSpec(memory_space=pltpu.SMEM)
     vmem = pl.BlockSpec(memory_space=pltpu.VMEM)
-    hbm = pl.BlockSpec(memory_space=pl.ANY)
+    hbm = pl.BlockSpec(memory_space=pltpu.HBM)
     shape = jax.ShapeDtypeStruct
     row, column = lax.axis_index("gy"), lax.axis_index("gz")
     first, last = row == 0, row == count_gy - 1
@@ -759,14 +792,13 @@
             pltpu.VMEM((24, ROWS, LANES), f32),
             pltpu.VMEM((24, ROWS, LANES), f32),
             pltpu.VMEM((96, LANES), f32),
-            pltpu.VMEM((96, LANES), f32),
         ],
     )
     below = lax.ppermute(up, "gy", [(i, (i + 1) % count_gy) for i in range(count_gy)])
     above = lax.ppermute(down, "gy", [((i + 1) % count_gy, i) for i in range(count_gy)])
     moved, back = call(
         third_kernel,
-        [lattice, tiles],
+        [lattice, shape((count_gz, 2, LANES), f32)],
         [info, next_pops, up, down, below, above],
         [smem] + [vmem] * 5,
         scratch=[

time: 68.9 us -> 68 us (0.987)
  blocking collectives: 42.6 us -> 41.3 us
    all_to_all x1, blocking collectives: 15 us -> 13.7 us  [body(): back = lax.all_to_all(back, 'gz', split_axis=0, concat_axis=0, tiled=True)]
where the time goes in v1:
time: 68 us; the launch traced here: 67.6 us
  blocking collectives  41.3 us (61%)
  starting transfers between devices  14.6 us (21%)
  Pallas kernels  7.17 us (11%)
  local copies, waits for them, and re-layouts  1.66 us (2%)
  waiting for transfers between devices  1.46 us (2%)
  between operations  1.4 us (2%)
    all_to_all x1, blocking collectives, body(): got = lax.all_to_all(send, 'gz', split_axis=0, concat_axis=0, tiled=True)  27.6 us
    all_to_all x1, blocking collectives, body(): back = lax.all_to_all(back, 'gz', split_axis=0, concat_axis=0, tiled=True)  13.7 us
    ppermute x1, starting transfers between devices, body(): lax.ppermute(down, 'gy', [((i + 1) % count_gy, i) for i in range(count_gy)])  12.7 us
    pallas_call x4, Pallas kernels, call(): pl.pallas_call(kernel, out_shape=out_shape, in_specs=in_specs, out_specs=...  7.17 us
    ppermute x1, starting transfers between devices, body(): lax.ppermute(up, 'gy', [(i, (i + 1) % count_gy) for i in range(count_gy)])  1.92 us
    unnamed x12, local copies, waits for them, and re-layouts  1.58 us
  transfers between devices with their start and end apart: 2, of which 2 were waited for; matrix products, arithmetic and copies ran while one was open for 0% of the time, Pallas kernels for 0%

profile of v1, /device:TPU:1, one launch (start us, length us, event | category | flops | bytes accessed | tf_op | source)
XLA Modules:
  0.0 67.6 jit_solution(12897900352703793823)
XLA Ops:
  0.7 0.0 copy-start.5
  1.3 0.0 copy-start.4
  1.3 0.0 copy-start.3
  1.4 0.0 copy-start.2
  1.4 0.1 stack.27.info_ref
  1.4 0.0 copy-done.5
  1.5 0.6 copy-done.4
  2.0 0.0 copy-done.3
  2.0 0.0 copy-done.2
  2.0 0.0 copy-start
  2.1 1.0 %copy-done = f32[19,4,8,128]{3,2,1,0:T(8,128)S(1)} copy-done((f32[19,4,8,128]{3,2,1,0:T(8,128)S(1)}, f32[19,4,8,128]{3,2,1,0:T(8,128)}, u32[]{:S(2)}) %copy-start) | copy-done | bytes 311320
  3.0 0.0 copy-start.1
  3.0 1.7 %shard_map.77 = (f32[32,8,128]{2,1,0:T(8,128)S(1)}, f32[1,512]{1,0:T(1,128)S(1)}, f32[96,128]{1,0:T(8,128)S(1)}, f32[4,8,128]{2,1,0:T(8,128)S(1)}, f32[4,8,128]{2,1,0:T(8,128)S(1)}) custom-call(s32[6]{0:T(128)S(1)} %stack.27.info_ref, s32[1]{0:T(128)S(6)} %copy.8.count_ref, s32[1,512]{1,0:T(1,128)S(1)} %bitcast.7, s32[3,512]{1,0:T(4,128)S(1)} %copy-done.3, ...), custom_call_target="tpu_custom_call" | custom-call | tf_op jit(solution)/shard_map/pallas_call | solution.py:78
  4.7 27.6 %all_to_all.10.got_ref = f32[32,8,128]{2,1,0:T(8,128)S(1)} all-to-all(f32[32,8,128]{2,1,0:T(8,128)S(1)} %get-tuple-element.12), channel_id=1, replica_groups=mesh['gy'=32,'gz'=32] {'gz'}, dimensions={0} | all-to-all | bytes 262144 | tf_op jit(solution)/shard_map/all_to_all | solution.py:783
  32.3 0.0 copy-done.1
  32.3 1.8 %shard_map.78 = (f32[19,4,8,128]{3,2,1,0:T(8,128)S(1)}, f32[160,128]{1,0:T(8,128)S(1)}, f32[160,128]{1,0:T(8,128)S(1)}) custom-call(s32[6]{0:T(128)S(1)} %stack.27.info_ref, f32[19,4,8,128]{3,2,1,0:T(8,128)S(1)} %copy-done.1, f32[32,8,128]{2,1,0:T(8,128)S(1)} %all_to_all.10.got_ref, f32[96,128]{1,0:T(8,128)S(1)} %get-tuple-element.13.field_ref, ...), custom_call_target="tpu_custom_call" | custom-call | tf_op jit(solution)/shard_map/pallas_call | solution.py:78
  34.0 1.9 %collective-permute-start = (f32[160,128]{1,0:T(8,128)S(1)}, f32[160,128]{1,0:T(8,128)S(1)}, u32[]{:S(2)}, u32[]{:S(2)}) collective-permute-start(f32[160,128]{1,0:T(8,128)S(1)} %get-tuple-element.17.up_ref), channel_id=1, source_target_pairs={{0,32},{32,64},{64,96},{96,128},{128,160},{160,192},{192,224},{224... | collective-permute-start | bytes 245768 | tf_op jit(solution)/shard_map/ppermute | solution.py:797
  36.0 12.7 %collective-permute-start.1 = (f32[160,128]{1,0:T(8,128)S(1)}, f32[160,128]{1,0:T(8,128)S(1)}, u32[]{:S(2)}, u32[]{:S(2)}) collective-permute-start(f32[160,128]{1,0:T(8,128)S(1)} %get-tuple-element.18.down_ref), channel_id=1, source_target_pairs={{32,0},{64,32},{96,64},{128,96},{160,128},{192,160},{224,192},{256... | collective-permute-start | bytes 245768 | tf_op jit(solution)/shard_map/ppermute | solution.py:798
  48.7 0.7 %collective-permute-done.below_ref = f32[160,128]{1,0:T(8,128)S(1)} collective-permute-done((f32[160,128]{1,0:T(8,128)S(1)}, f32[160,128]{1,0:T(8,128)S(1)}, u32[]{:S(2)}, u32[]{:S(2)}) %collective-permute-start) | collective-permute-done | bytes 81952 | tf_op jit(solution)/shard_map/ppermute | solution.py:797
  49.4 0.7 %collective-permute-done.1.above_ref = f32[160,128]{1,0:T(8,128)S(1)} collective-permute-done((f32[160,128]{1,0:T(8,128)S(1)}, f32[160,128]{1,0:T(8,128)S(1)}, u32[]{:S(2)}, u32[]{:S(2)}) %collective-permute-start.1) | collective-permute-done | bytes 81952 | tf_op jit(solution)/shard_map/ppermute | solution.py:798
  50.1 2.3 %shard_map.79 = (f32[19,4,8,128]{3,2,1,0:T(8,128)S(1)}, f32[32,2,128]{2,1,0:T(2,128)S(1)}) custom-call(s32[6]{0:T(128)S(1)} %stack.27.info_ref, f32[19,4,8,128]{3,2,1,0:T(8,128)S(1)} %get-tuple-element.16.next_ref, f32[160,128]{1,0:T(8,128)S(1)} %get-tuple-element.17.up_ref, f32[160,128]{1,0:T(8,128)S(1)} %get-tuple-element.18.down_ref, ...), custom_call_target="tpu_custom_call" | custom-call | tf_op jit(solution)/shard_map/pallas_call | solution.py:78
  52.4 13.7 %all_to_all.11.got_ref = f32[32,2,128]{2,1,0:T(2,128)S(1)} all-to-all(f32[32,2,128]{2,1,0:T(2,128)S(1)} %get-tuple-element.20), channel_id=1, replica_groups=mesh['gy'=32,'gz'=32] {'gz'}, dimensions={0} | all-to-all | bytes 65536 | tf_op jit(solution)/shard_map/all_to_all | solution.py:812
  66.1 1.5 %shard_map.80 = (f32[19,4,8,128]{3,2,1,0:T(8,128)}, f32[3,512]{1,0:T(4,128)}) custom-call(s32[6]{0:T(128)S(1)} %stack.27.info_ref, s32[1]{0:T(128)S(6)} %copy.8.count_ref, f32[19,4,8,128]{3,2,1,0:T(8,128)S(1)} %get-tuple-element.19.moved_ref, f32[32,2,128]{2,1,0:T(2,128)S(1)} %all_to_all.11.got_ref, s32[1,512]{1,0:T(1,128)S(1)} %bitcast.8, ...), custom_call_target="tpu_custom_call" | custom-call | tf_op jit(solution)/shard_map/pallas_call | solution.py:78
Async XLA Ops:
  0.7 0.8 %copy-start.5 = (f32[3,512]{1,0:T(4,128)S(1)}, f32[3,512]{1,0:T(4,128)}, u32[]{:S(2)}) copy-start(f32[3,512]{1,0:T(4,128)} %speed_hbm.1) | copy-start | bytes 18436
  1.3 0.7 %copy-start.4 = (f32[3,512]{1,0:T(4,128)S(1)}, f32[3,512]{1,0:T(4,128)}, u32[]{:S(2)}) copy-start(f32[3,512]{1,0:T(4,128)} %frac_hbm.1) | copy-start | bytes 18436
  1.3 0.7 %copy-start.3 = (s32[3,512]{1,0:T(4,128)S(1)}, s32[3,512]{1,0:T(4,128)}, u32[]{:S(2)}) copy-start(s32[3,512]{1,0:T(4,128)} %cell_hbm.1) | copy-start | bytes 18436
  1.4 0.7 %copy-start.2 = (s32[512,1]{0,1:T(1,128)S(1)}, s32[512,1]{0,1:T(1,128)}, u32[]{:S(2)}) copy-start(s32[512,1]{0,1:T(1,128)} %param.7) | copy-start | bytes 6148
  2.0 1.0 %copy-start = (f32[19,4,8,128]{3,2,1,0:T(8,128)S(1)}, f32[19,4,8,128]{3,2,1,0:T(8,128)}, u32[]{:S(2)}) copy-start(f32[19,4,8,128]{3,2,1,0:T(8,128)} %pops_ref.1) | copy-start | bytes 933892
  3.0 29.3 %copy-start.1 = (f32[19,4,8,128]{3,2,1,0:T(8,128)S(1)}, f32[19,4,8,128]{3,2,1,0:T(8,128)}, u32[]{:S(2)}) copy-start(f32[19,4,8,128]{3,2,1,0:T(8,128)} %pops_ref.1) | copy-start | bytes 933892
  34.0 15.4 %collective-permute-start = (f32[160,128]{1,0:T(8,128)S(1)}, f32[160,128]{1,0:T(8,128)S(1)}, u32[]{:S(2)}, u32[]{:S(2)}) collective-permute-start(f32[160,128]{1,0:T(8,128)S(1)} %get-tuple-element.17.up_ref), channel_id=1, source_target_pairs={{0,32},{32,64},{64,96},{96,128},{128,160},{160,192},{192,224},{224... | collective-permute-start | bytes 245768 | tf_op jit(solution)/shard_map/ppermute | solution.py:797
  36.0 14.2 %collective-permute-start.1 = (f32[160,128]{1,0:T(8,128)S(1)}, f32[160,128]{1,0:T(8,128)S(1)}, u32[]{:S(2)}, u32[]{:S(2)}) collective-permute-start(f32[160,128]{1,0:T(8,128)S(1)} %get-tuple-element.18.down_ref), channel_id=1, source_target_pairs={{32,0},{64,32},{96,64},{128,96},{160,128},{192,160},{224,192},{256... | collective-permute-start | bytes 245768 | tf_op jit(solution)/shard_map/ppermute | solution.py:798

commit v2 on v1

--- a/solution.py
+++ b/solution.py
@@ -73,17 +73,34 @@
     return high, (value - high.astype(f32)).astype(bf16)
 
 
-def call(kernel, out_shape, args, in_specs, scratch=()):
+def call(kernel, out_shape, args, in_specs, scratch=(), out_specs=None, aliases=()):
     vmem = pl.BlockSpec(memory_space=pltpu.VMEM)
     return pl.pallas_call(
         kernel,
         out_shape=out_shape,
         in_specs=in_specs,
-        out_specs=[vmem] * len(out_shape),
+        out_specs=out_specs or [vmem] * len(out_shape),
+        input_output_aliases=dict(aliases),
         scratch_shapes=list(scratch),
         compiler_params=pltpu.CompilerParams(vmem_limit_bytes=32 * 1024 * 1024),
         interpret=INTERPRET,
     )(*args)
+
+
+def z_neighbours():
+    column, size = lax.axis_index("gz"), lax.axis_size("gz")
+    return (column + size - 1) % size, (column + 1) % size
+
+
+def y_ends():
+    place, size = lax.axis_index("gy"), lax.axis_size("gy")
+    first, last = place == 0, place == size - 1
+    return (
+        jnp.where(first, -1, 0),
+        jnp.where(last, -1, ROWS - 1),
+        jnp.where(first, 0, -1),
+        jnp.where(last, ROWS - 1, -1),
+    )
 
 
 def moments_of(pops):
@@ -219,8 +236,8 @@
 
 
 def first_kernel(
-    info_ref, count_ref, owner_hbm, cell_hbm, frac_hbm, speed_hbm, pops_hbm,
-    send_ref, rank_ref, field_ref, density_ref, relax_ref,
+    count_ref, owner_hbm, cell_hbm, frac_hbm, speed_hbm, pops_hbm,
+    send_ref, rank_ref, live_ref, field_ref, density_ref, relax_ref,
     owner_ref, cell_ref, frac_ref, speed_ref, pops_ref, sems,
 ):
     copies = [
@@ -240,8 +257,9 @@
     for copy in copies[0:4]:
         copy.wait()
     owners, markers = send_ref.shape[0], owner_ref.shape[1]
-    live = iota((1, markers), 1) < count_ref[0]
+    live = iota((1, markers), 1) < count_ref[...]
     owner = jnp.where(live, owner_ref[...], -1)
+    live_ref[...] = owner
     base_z = cell_ref[2:3, :]
     upper, lower = base_z == LANES - 2, base_z == 0
     twin = jnp.where(
@@ -254,18 +272,23 @@
     hits = jnp.concatenate(
         [hit.astype(f32), (hit & upper).astype(f32), (hit & lower).astype(f32)], 0
     )
-    below = (iota((LANES, LANES), 0) < iota((LANES, LANES), 1)).astype(bf16)
-    before = jnp.zeros((3 * owners, 1), f32)
+    blocks = markers // LANES
+    parts = [hits[:, block * LANES : (block + 1) * LANES] for block in range(blocks)]
+    earlier = iota((LANES, 2 * LANES), 0) < iota((LANES, 2 * LANES), 1)
+    counts = jnp.dot(
+        jnp.concatenate(parts, 0).astype(bf16), earlier.astype(bf16), preferred_element_type=f32
+    )
+    before = None
     ranks = [[], [], []]
-    for start in range(0, markers, LANES):
-        part = hits[:, start : start + LANES]
-        inner = jnp.dot(part.astype(bf16), below, preferred_element_type=f32)
-        picked = part * (inner + before)
+    for block in range(blocks):
+        inner = counts[block * 3 * owners : (block + 1) * 3 * owners]
+        place = inner[:, 0:LANES] if before is None else inner[:, 0:LANES] + before
+        before = inner[:, LANES:] if before is None else inner[:, LANES:] + before
+        picked = parts[block] * place
         for kind in range(3):
             ranks[kind].append(
                 jnp.sum(picked[kind * owners : (kind + 1) * owners], 0, keepdims=True)
             )
-        before = before + jnp.sum(part, 1, keepdims=True)
     rank, rank_up, rank_low = [jnp.concatenate(kind, 1) for kind in ranks]
     rank_ref[...] = rank
     lane_up = jnp.where(rank_up < FEW, SLOTS + rank_up, FIRST_SPARE - FEW + rank_up)
@@ -302,6 +325,7 @@
     send_ref[...] = tiles.reshape(owners, 8, LANES)
 
     copies[4].wait()
+
     lane = iota((ROWS, LANES), 1)
     to_right, to_left = jnp.zeros((ROWS, LANES), f32), jnp.zeros((ROWS, LANES), f32)
     for plane in range(PLANES):
@@ -325,17 +349,17 @@
             here = lane == place
             to_right = jnp.where(here, roll(right, place - (LANES - 1) + shift, 1), to_right)
             to_left = jnp.where(here, roll(left, place - shift, 1), to_left)
-    left, right = info_ref[0], info_ref[1]
+    left, right = z_neighbours()
     send_ref[left] = send_ref[left] + to_left
     send_ref[right] = send_ref[right] + to_right
 
 
 def second_kernel(
-    info_ref, pops_ref, got_ref, field_ref, density_ref, relax_ref,
+    pops_ref, got_ref, field_ref, density_ref, relax_ref,
     next_ref, up_ref, down_ref,
     post_ref, near_ref, far_ref, twin_ref,
 ):
-    left, right = info_ref[0], info_ref[1]
+    left, right = z_neighbours()
     lane = iota((ROWS, LANES), 1)
     row = iota((ROWS, LANES), 0)
     sources = got_ref.shape[0]
@@ -518,11 +542,12 @@
 
 
 def third_kernel(
-    info_ref, next_ref, up_ref, down_ref, below_ref, above_ref,
+    next_ref, up_ref, down_ref, below_ref, above_ref,
     moved_ref, back_ref,
     wide_ref, field_ref, density_ref, post_ref, outer_ref,
 ):
-    left, right, first_open, last_open, first_wall, last_wall = [info_ref[i] for i in range(6)]
+    left, right = z_neighbours()
+    first_open, last_open, first_wall, last_wall = y_ends()
     lane = iota((ROWS, LANES), 1)
     row = iota((ROWS, LANES), 0)
     sources = back_ref.shape[0]
@@ -690,8 +715,11 @@
         back_ref[target, 1:2, :] = jnp.sum(early, 0, keepdims=True)
 
 
-def last_kernel(info_ref, count_ref, moved_ref, got_ref, owner_ref, rank_ref, pops_ref, force_ref):
-    left, right, _, _, first_wall, last_wall = [info_ref[i] for i in range(6)]
+def last_kernel(
+    moved_ref, got_ref, owner_ref, rank_ref, pops_ref, force_ref
+):
+    left, right = z_neighbours()
+    _, _, first_wall, last_wall = y_ends()
     lane = iota((ROWS, LANES), 1)
     row = iota((ROWS, LANES), 0)
 
@@ -706,26 +734,26 @@
         return face
 
     from_left, from_right = face_of(left), face_of(right)
+    changed = [i for i in range(19) if velocity_table[i][2]]
     for member in range(19):
+        if member not in changed:
+            pops_ref[member] = moved_ref[member]
+    for number, member in enumerate(changed):
         _, shift_y, shift_z = velocity_table[member]
         for plane in range(PLANES):
-            value = moved_ref[member, plane]
-            if shift_z:
-                if shift_z == 1:
-                    place = ahead_z.index(member) * PLANES + plane
-                    edge, here = roll(from_left, -place, 1), lane == 0
-                else:
-                    place = back_z.index(member) * PLANES + plane
-                    edge, here = roll(from_right, LANES - 1 - place, 1), lane == LANES - 1
-                if shift_y == 1:
-                    here = here & (row != first_wall)
-                if shift_y == -1:
-                    here = here & (row != last_wall)
-                value = jnp.where(here, edge, value)
-            pops_ref[member, plane] = value
+            if shift_z == 1:
+                place = ahead_z.index(member) * PLANES + plane
+                edge, here = roll(from_left, -place, 1), lane == 0
+            else:
+                place = back_z.index(member) * PLANES + plane
+                edge, here = roll(from_right, LANES - 1 - place, 1), lane == LANES - 1
+            if shift_y == 1:
+                here = here & (row != first_wall)
+            if shift_y == -1:
+                here = here & (row != last_wall)
+            pops_ref[member, plane] = jnp.where(here, edge, moved_ref[member, plane])
     owners, markers = got_ref.shape[0], owner_ref.shape[1]
-    live = iota((1, markers), 1) < count_ref[0]
-    owner = jnp.where(live, owner_ref[...], -1)
+    owner = owner_ref[...]
     spot = (iota((LANES, markers), 0).astype(f32) == rank_ref[...]).astype(bf16)
     rows = got_ref[:, 0, :]
     high, low = split_two(
@@ -745,48 +773,35 @@
 def body(populations, marker_owner, marker_cell, marker_frac, marker_speed, marker_count):
     count_gy, count_gz = lax.axis_size("gy"), lax.axis_size("gz")
     markers = marker_owner.shape[0]
-    smem = pl.BlockSpec(memory_space=pltpu.SMEM)
     vmem = pl.BlockSpec(memory_space=pltpu.VMEM)
-    hbm = pl.BlockSpec(memory_space=pltpu.HBM)
     shape = jax.ShapeDtypeStruct
-    row, column = lax.axis_index("gy"), lax.axis_index("gz")
-    first, last = row == 0, row == count_gy - 1
-    info = jnp.stack(
-        [
-            (column + count_gz - 1) % count_gz,
-            (column + 1) % count_gz,
-            jnp.where(first, -1, 0),
-            jnp.where(last, -1, ROWS - 1),
-            jnp.where(first, 0, -1),
-            jnp.where(last, ROWS - 1, -1),
-        ]
-    ).astype(jnp.int32)
-    owner = marker_owner.reshape(1, markers)
     tiles = shape((count_gz, 8, LANES), f32)
     field = shape((96, LANES), f32)
     cells = shape((PLANES, ROWS, LANES), f32)
     lattice = shape(populations.shape, f32)
-    send, rank, speeds, density, relax = call(
+    inputs = [
+        marker_owner.reshape(1, markers),
+        marker_cell,
+        marker_frac,
+        marker_speed,
+        populations,
+    ]
+    send, rank, live, speeds, density, relax = call(
         first_kernel,
-        [tiles, shape((1, markers), f32), field, cells, cells],
-        [info, marker_count, owner, marker_cell, marker_frac, marker_speed, populations],
-        [smem] * 2 + [hbm] * 5,
-        scratch=[
-            pltpu.VMEM((1, markers), jnp.int32),
-            pltpu.VMEM((3, markers), jnp.int32),
-            pltpu.VMEM((3, markers), f32),
-            pltpu.VMEM((3, markers), f32),
-            pltpu.VMEM(populations.shape, f32),
-            pltpu.SemaphoreType.DMA((5,)),
-        ],
+        [tiles, shape((1, markers), f32), shape((1, markers), jnp.int32), field, cells, cells],
+        [marker_count.reshape(1, 1)]
+        + [pltpu.with_memory_space_constraint(value, pltpu.HBM) for value in inputs],
+        [vmem] + [pl.BlockSpec(memory_space=pltpu.HBM)] * 5,
+        scratch=[pltpu.VMEM(value.shape, value.dtype) for value in inputs]
+        + [pltpu.SemaphoreType.DMA((5,))],
     )
     got = lax.all_to_all(send, "gz", split_axis=0, concat_axis=0, tiled=True)
     face = shape((FACE_ROWS, LANES), f32)
     next_pops, up, down = call(
         second_kernel,
         [lattice, face, face],
-        [info, populations, got, speeds, density, relax],
-        [smem] + [vmem] * 5,
+        [populations, got, speeds, density, relax],
+        [vmem] * 5,
         scratch=[
             pltpu.VMEM(populations.shape, f32),
             pltpu.VMEM((24, ROWS, LANES), f32),
@@ -799,8 +814,8 @@
     moved, back = call(
         third_kernel,
         [lattice, shape((count_gz, 2, LANES), f32)],
-        [info, next_pops, up, down, below, above],
-        [smem] + [vmem] * 5,
+        [next_pops, up, down, below, above],
+        [vmem] * 5,
         scratch=[
             pltpu.VMEM(populations.shape, f32),
             pltpu.VMEM((96, LANES), f32),
@@ -813,8 +828,8 @@
     pops, force = call(
         last_kernel,
         [lattice, shape((3, markers), f32)],
-        [info, marker_count, moved, back, owner, rank],
-        [smem] * 2 + [vmem] * 4,
+        [moved, back, live, rank],
+        [vmem] * 4,
     )
     return pops, force
 

time: 68 us -> 64.8 us (0.953)
  local copies, waits for them, and re-layouts: 1.66 us -> 0.01 us
  Pallas kernels: 7.17 us -> 5.75 us
    unnamed x12 -> x2, local copies, waits for them, and re-layouts: 1.58 us -> 0.01 us
    pallas_call x4, Pallas kernels: 7.17 us -> 5.75 us  [call(): pl.pallas_call(kernel, out_shape=out_shape, in_specs=in_specs, out_specs=...]
where the time goes in v2:
time: 64.8 us; the launch traced here: 64.5 us
  blocking collectives  41.3 us (64%)
  starting transfers between devices  14.6 us (23%)
  Pallas kernels  5.75 us (9%)
  waiting for transfers between devices  1.46 us (2%)
  between operations  1.37 us (2%)
    all_to_all x1, blocking collectives, body(): got = lax.all_to_all(send, 'gz', split_axis=0, concat_axis=0, tiled=True)  27.6 us
    all_to_all x1, blocking collectives, body(): back = lax.all_to_all(back, 'gz', split_axis=0, concat_axis=0, tiled=True)  13.7 us
    ppermute x1, starting transfers between devices, body(): lax.ppermute(down, 'gy', [((i + 1) % count_gy, i) for i in range(count_gy)])  12.7 us
    pallas_call x4, Pallas kernels, call(): pl.pallas_call(kernel, out_shape=out_shape, in_specs=in_specs, out_specs=...  5.75 us
    ppermute x1, starting transfers between devices, body(): lax.ppermute(up, 'gy', [(i, (i + 1) % count_gy) for i in range(count_gy)])  1.92 us
  transfers between devices with their start and end apart: 2, of which 2 were waited for; matrix products, arithmetic and copies ran while one was open for 0% of the time, Pallas kernels for 0%

profile of v2, /device:TPU:1, one launch (start us, length us, event | category | flops | bytes accessed | tf_op | source)
XLA Modules:
  0.0 64.5 jit_solution(14254174628671867343)
XLA Ops:
  0.6 0.0 copy-start
  1.3 1.9 %shard_map.77 = (f32[32,8,128]{2,1,0:T(8,128)S(1)}, f32[1,512]{1,0:T(1,128)S(1)}, s32[1,512]{1,0:T(1,128)S(1)}, f32[96,128]{1,0:T(8,128)S(1)}, f32[4,8,128]{2,1,0:T(8,128)S(1)}, /*index=5*/f32[4,8,128]{2,1,0:T(8,128)S(1)}) custom-call(s32[1,1]{1,0:T(1,128)} %bitcast.2.count_ref, s32[1,512]{1,0:T(1,128)} %bitcast.3, s32[3,512]{1,0:T(4,128)} %cell_hbm.1, ...), custom_call_target="tpu_custom_call" | custom-call | tf_op jit(solution)/shard_map/pallas_call | solution.py:78
  3.2 27.6 %all_to_all.10.got_ref = f32[32,8,128]{2,1,0:T(8,128)S(1)} all-to-all(f32[32,8,128]{2,1,0:T(8,128)S(1)} %get-tuple-element.13), channel_id=1, replica_groups=mesh['gy'=32,'gz'=32] {'gz'}, dimensions={0} | all-to-all | bytes 262144 | tf_op jit(solution)/shard_map/all_to_all | solution.py:798
  30.8 0.0 copy-done
  30.8 1.2 %shard_map.78 = (f32[19,4,8,128]{3,2,1,0:T(8,128)S(1)}, f32[160,128]{1,0:T(8,128)S(1)}, f32[160,128]{1,0:T(8,128)S(1)}) custom-call(f32[19,4,8,128]{3,2,1,0:T(8,128)S(1)} %copy-done, f32[32,8,128]{2,1,0:T(8,128)S(1)} %all_to_all.10.got_ref, f32[96,128]{1,0:T(8,128)S(1)} %get-tuple-element.14.field_ref, f32[4,8,128]{2,1,0:T(8,128)S(1)} %get-tuple-element.15.density_ref, ...), custom_call_target="tpu_custom_call" | custom-call | tf_op jit(solution)/shard_map/pallas_call | solution.py:78
  32.0 1.9 %collective-permute-start = (f32[160,128]{1,0:T(8,128)S(1)}, f32[160,128]{1,0:T(8,128)S(1)}, u32[]{:S(2)}, u32[]{:S(2)}) collective-permute-start(f32[160,128]{1,0:T(8,128)S(1)} %get-tuple-element.18.up_ref), channel_id=1, source_target_pairs={{0,32},{32,64},{64,96},{96,128},{128,160},{160,192},{192,224},{224... | collective-permute-start | bytes 245768 | tf_op jit(solution)/shard_map/ppermute | solution.py:812
  33.9 12.7 %collective-permute-start.1 = (f32[160,128]{1,0:T(8,128)S(1)}, f32[160,128]{1,0:T(8,128)S(1)}, u32[]{:S(2)}, u32[]{:S(2)}) collective-permute-start(f32[160,128]{1,0:T(8,128)S(1)} %get-tuple-element.19.down_ref), channel_id=1, source_target_pairs={{32,0},{64,32},{96,64},{128,96},{160,128},{192,160},{224,192},{256... | collective-permute-start | bytes 245768 | tf_op jit(solution)/shard_map/ppermute | solution.py:813
  46.6 0.7 %collective-permute-done.below_ref = f32[160,128]{1,0:T(8,128)S(1)} collective-permute-done((f32[160,128]{1,0:T(8,128)S(1)}, f32[160,128]{1,0:T(8,128)S(1)}, u32[]{:S(2)}, u32[]{:S(2)}) %collective-permute-start) | collective-permute-done | bytes 81952 | tf_op jit(solution)/shard_map/ppermute | solution.py:812
  47.4 0.7 %collective-permute-done.1.above_ref = f32[160,128]{1,0:T(8,128)S(1)} collective-permute-done((f32[160,128]{1,0:T(8,128)S(1)}, f32[160,128]{1,0:T(8,128)S(1)}, u32[]{:S(2)}, u32[]{:S(2)}) %collective-permute-start.1) | collective-permute-done | bytes 81952 | tf_op jit(solution)/shard_map/ppermute | solution.py:813
  48.1 1.7 %shard_map.79 = (f32[19,4,8,128]{3,2,1,0:T(8,128)S(1)}, f32[32,2,128]{2,1,0:T(2,128)S(1)}) custom-call(f32[19,4,8,128]{3,2,1,0:T(8,128)S(1)} %get-tuple-element.17.next_ref, f32[160,128]{1,0:T(8,128)S(1)} %get-tuple-element.18.up_ref, f32[160,128]{1,0:T(8,128)S(1)} %get-tuple-element.19.down_ref, f32[160,128]{1,0:T(8,128)S(1)} %collective-permute-done.below_ref, ...), custom_call_target="tpu_custom_call" | custom-call | tf_op jit(solution)/shard_map/pallas_call | solution.py:78
  49.8 13.7 %all_to_all.11.got_ref = f32[32,2,128]{2,1,0:T(2,128)S(1)} all-to-all(f32[32,2,128]{2,1,0:T(2,128)S(1)} %get-tuple-element.21), channel_id=1, replica_groups=mesh['gy'=32,'gz'=32] {'gz'}, dimensions={0} | all-to-all | bytes 65536 | tf_op jit(solution)/shard_map/all_to_all | solution.py:827
  63.5 1.0 %shard_map.80 = (f32[19,4,8,128]{3,2,1,0:T(8,128)}, f32[3,512]{1,0:T(4,128)}) custom-call(f32[19,4,8,128]{3,2,1,0:T(8,128)S(1)} %get-tuple-element.20.moved_ref, f32[32,2,128]{2,1,0:T(2,128)S(1)} %all_to_all.11.got_ref, s32[1,512]{1,0:T(1,128)S(1)} %get-tuple-element.22.owner_ref, f32[1,512]{1,0:T(1,128)S(1)} %get-tuple-element.23.rank_ref), custom_call_target="tpu_custom_call" | custom-call | tf_op jit(solution)/shard_map/pallas_call | solution.py:78
Async XLA Ops:
  0.6 30.2 %copy-start = (f32[19,4,8,128]{3,2,1,0:T(8,128)S(1)}, f32[19,4,8,128]{3,2,1,0:T(8,128)}, u32[]{:S(2)}) copy-start(f32[19,4,8,128]{3,2,1,0:T(8,128)} %pops_ref.1) | copy-start | bytes 933892
  32.0 15.4 %collective-permute-start = (f32[160,128]{1,0:T(8,128)S(1)}, f32[160,128]{1,0:T(8,128)S(1)}, u32[]{:S(2)}, u32[]{:S(2)}) collective-permute-start(f32[160,128]{1,0:T(8,128)S(1)} %get-tuple-element.18.up_ref), channel_id=1, source_target_pairs={{0,32},{32,64},{64,96},{96,128},{128,160},{160,192},{192,224},{224... | collective-permute-start | bytes 245768 | tf_op jit(solution)/shard_map/ppermute | solution.py:812
  33.9 14.2 %collective-permute-start.1 = (f32[160,128]{1,0:T(8,128)S(1)}, f32[160,128]{1,0:T(8,128)S(1)}, u32[]{:S(2)}, u32[]{:S(2)}) collective-permute-start(f32[160,128]{1,0:T(8,128)S(1)} %get-tuple-element.19.down_ref), channel_id=1, source_target_pairs={{32,0},{64,32},{96,64},{128,96},{160,128},{192,160},{224,192},{256... | collective-permute-start | bytes 245768 | tf_op jit(solution)/shard_map/ppermute | solution.py:813

commit v3 on v2

--- a/solution.py
+++ b/solution.py
@@ -573,6 +573,7 @@
             at = axis_no * 32 + plane * 8
             field_ref[at : at + 8, :] = speeds[axis_no]
 
+    outside = ((row < PLANES) & (first_wall == 0)) | ((row >= PLANES) & (last_wall > 0))
     outer = []
     for member in range(19):
         if member in falling:
@@ -583,7 +584,8 @@
             top = four(up_ref, AT_NEXT + rising.index(member) * PLANES)
         else:
             top = four(above_ref, AT_POPS + (level + falling).index(member) * PLANES)
-        outer.append(jnp.concatenate([low, top], 0))
+        value = jnp.concatenate([low, top], 0)
+        outer.append(jnp.where(outside, 0.0 if member else 1.0, value))
     outer_density, outer_speeds = moments_of(outer)
     lows, tops = [], []
     for axis_no in range(3):
@@ -809,8 +811,8 @@
             pltpu.VMEM((96, LANES), f32),
         ],
     )
-    below = lax.ppermute(up, "gy", [(i, (i + 1) % count_gy) for i in range(count_gy)])
-    above = lax.ppermute(down, "gy", [((i + 1) % count_gy, i) for i in range(count_gy)])
+    below = lax.ppermute(up, "gy", [(i, i + 1) for i in range(count_gy - 1)])
+    above = lax.ppermute(down, "gy", [(i + 1, i) for i in range(count_gy - 1)])
     moved, back = call(
         third_kernel,
         [lattice, shape((count_gz, 2, LANES), f32)],

time: 64.8 us -> 63.4 us (0.978)
  the two profiles are of different devices: /device:TPU:1 before, /device:TPU:9 now
where the time goes in v3:
time: 63.4 us; the launch traced here: 63.1 us
  blocking collectives  33.5 us (53%)
  starting transfers between devices  20.9 us (33%)
  Pallas kernels  5.77 us (9%)
  waiting for transfers between devices  1.63 us (3%)
  between operations  1.37 us (2%)
    all_to_all x1, blocking collectives, body(): got = lax.all_to_all(send, 'gz', split_axis=0, concat_axis=0, tiled=True)  19.8 us
    ppermute x1, starting transfers between devices, body(): above = lax.ppermute(down, 'gy', [(i + 1, i) for i in range(count_gy - 1)])  16.2 us
    all_to_all x1, blocking collectives, body(): back = lax.all_to_all(back, 'gz', split_axis=0, concat_axis=0, tiled=True)  13.7 us
    pallas_call x4, Pallas kernels, call(): pl.pallas_call(kernel, out_shape=out_shape, in_specs=in_specs, out_specs=...  5.77 us
    ppermute x1, starting transfers between devices, body(): below = lax.ppermute(up, 'gy', [(i, i + 1) for i in range(count_gy - 1)])  4.67 us
  transfers between devices with their start and end apart: 2, of which 2 were waited for; matrix products, arithmetic and copies ran while one was open for 0% of the time, Pallas kernels for 0%

profile of v3, /device:TPU:9, one launch (start us, length us, event | category | flops | bytes accessed | tf_op | source)
XLA Modules:
  0.0 63.1 jit_solution(10460011912552701511)
XLA Ops:
  0.6 0.0 copy-start
  1.3 1.9 %shard_map.77 = (f32[32,8,128]{2,1,0:T(8,128)S(1)}, f32[1,512]{1,0:T(1,128)S(1)}, s32[1,512]{1,0:T(1,128)S(1)}, f32[96,128]{1,0:T(8,128)S(1)}, f32[4,8,128]{2,1,0:T(8,128)S(1)}, /*index=5*/f32[4,8,128]{2,1,0:T(8,128)S(1)}) custom-call(s32[1,1]{1,0:T(1,128)} %bitcast.2.count_ref, s32[1,512]{1,0:T(1,128)} %bitcast.3, s32[3,512]{1,0:T(4,128)} %cell_hbm.1, ...), custom_call_target="tpu_custom_call" | custom-call | tf_op jit(solution)/shard_map/pallas_call | solution.py:78
  3.2 19.8 %all_to_all.10.got_ref = f32[32,8,128]{2,1,0:T(8,128)S(1)} all-to-all(f32[32,8,128]{2,1,0:T(8,128)S(1)} %get-tuple-element.13), channel_id=1, replica_groups=mesh['gy'=32,'gz'=32] {'gz'}, dimensions={0} | all-to-all | bytes 262144 | tf_op jit(solution)/shard_map/all_to_all | solution.py:800
  23.0 0.0 copy-done
  23.0 1.2 %shard_map.78 = (f32[19,4,8,128]{3,2,1,0:T(8,128)S(1)}, f32[160,128]{1,0:T(8,128)S(1)}, f32[160,128]{1,0:T(8,128)S(1)}) custom-call(f32[19,4,8,128]{3,2,1,0:T(8,128)S(1)} %copy-done, f32[32,8,128]{2,1,0:T(8,128)S(1)} %all_to_all.10.got_ref, f32[96,128]{1,0:T(8,128)S(1)} %get-tuple-element.14.field_ref, f32[4,8,128]{2,1,0:T(8,128)S(1)} %get-tuple-element.15.density_ref, ...), custom_call_target="tpu_custom_call" | custom-call | tf_op jit(solution)/shard_map/pallas_call | solution.py:78
  24.2 4.7 %collective-permute-start = (f32[160,128]{1,0:T(8,128)S(1)}, f32[160,128]{1,0:T(8,128)S(1)}, u32[]{:S(2)}, u32[]{:S(2)}) collective-permute-start(f32[160,128]{1,0:T(8,128)S(1)} %get-tuple-element.18.up_ref), channel_id=1, source_target_pairs={{0,32},{32,64},{64,96},{96,128},{128,160},{160,192},{192,224},{224... | collective-permute-start | bytes 245768 | tf_op jit(solution)/shard_map/ppermute | solution.py:814
  28.9 16.2 %collective-permute-start.1 = (f32[160,128]{1,0:T(8,128)S(1)}, f32[160,128]{1,0:T(8,128)S(1)}, u32[]{:S(2)}, u32[]{:S(2)}) collective-permute-start(f32[160,128]{1,0:T(8,128)S(1)} %get-tuple-element.19.down_ref), channel_id=1, source_target_pairs={{32,0},{64,32},{96,64},{128,96},{160,128},{192,160},{224,192},{256... | collective-permute-start | bytes 245768 | tf_op jit(solution)/shard_map/ppermute | solution.py:815
  45.1 0.8 %collective-permute-done.below_ref = f32[160,128]{1,0:T(8,128)S(1)} collective-permute-done((f32[160,128]{1,0:T(8,128)S(1)}, f32[160,128]{1,0:T(8,128)S(1)}, u32[]{:S(2)}, u32[]{:S(2)}) %collective-permute-start) | collective-permute-done | bytes 81952 | tf_op jit(solution)/shard_map/ppermute | solution.py:814
  45.9 0.9 %collective-permute-done.1.above_ref = f32[160,128]{1,0:T(8,128)S(1)} collective-permute-done((f32[160,128]{1,0:T(8,128)S(1)}, f32[160,128]{1,0:T(8,128)S(1)}, u32[]{:S(2)}, u32[]{:S(2)}) %collective-permute-start.1) | collective-permute-done | bytes 81952 | tf_op jit(solution)/shard_map/ppermute | solution.py:815
  46.8 1.7 %shard_map.79 = (f32[19,4,8,128]{3,2,1,0:T(8,128)S(1)}, f32[32,2,128]{2,1,0:T(2,128)S(1)}) custom-call(f32[19,4,8,128]{3,2,1,0:T(8,128)S(1)} %get-tuple-element.17.next_ref, f32[160,128]{1,0:T(8,128)S(1)} %get-tuple-element.18.up_ref, f32[160,128]{1,0:T(8,128)S(1)} %get-tuple-element.19.down_ref, f32[160,128]{1,0:T(8,128)S(1)} %collective-permute-done.below_ref, ...), custom_call_target="tpu_custom_call" | custom-call | tf_op jit(solution)/shard_map/pallas_call | solution.py:78
  48.5 13.7 %all_to_all.11.got_ref = f32[32,2,128]{2,1,0:T(2,128)S(1)} all-to-all(f32[32,2,128]{2,1,0:T(2,128)S(1)} %get-tuple-element.21), channel_id=1, replica_groups=mesh['gy'=32,'gz'=32] {'gz'}, dimensions={0} | all-to-all | bytes 65536 | tf_op jit(solution)/shard_map/all_to_all | solution.py:829
  62.2 1.0 %shard_map.80 = (f32[19,4,8,128]{3,2,1,0:T(8,128)}, f32[3,512]{1,0:T(4,128)}) custom-call(f32[19,4,8,128]{3,2,1,0:T(8,128)S(1)} %get-tuple-element.20.moved_ref, f32[32,2,128]{2,1,0:T(2,128)S(1)} %all_to_all.11.got_ref, s32[1,512]{1,0:T(1,128)S(1)} %get-tuple-element.22.owner_ref, f32[1,512]{1,0:T(1,128)S(1)} %get-tuple-element.23.rank_ref), custom_call_target="tpu_custom_call" | custom-call | tf_op jit(solution)/shard_map/pallas_call | solution.py:78
Async XLA Ops:
  0.6 22.4 %copy-start = (f32[19,4,8,128]{3,2,1,0:T(8,128)S(1)}, f32[19,4,8,128]{3,2,1,0:T(8,128)}, u32[]{:S(2)}) copy-start(f32[19,4,8,128]{3,2,1,0:T(8,128)} %pops_ref.1) | copy-start | bytes 933892
  24.2 21.7 %collective-permute-start = (f32[160,128]{1,0:T(8,128)S(1)}, f32[160,128]{1,0:T(8,128)S(1)}, u32[]{:S(2)}, u32[]{:S(2)}) collective-permute-start(f32[160,128]{1,0:T(8,128)S(1)} %get-tuple-element.18.up_ref), channel_id=1, source_target_pairs={{0,32},{32,64},{64,96},{96,128},{128,160},{160,192},{192,224},{224... | collective-permute-start | bytes 245768 | tf_op jit(solution)/shard_map/ppermute | solution.py:814
  28.9 17.9 %collective-permute-start.1 = (f32[160,128]{1,0:T(8,128)S(1)}, f32[160,128]{1,0:T(8,128)S(1)}, u32[]{:S(2)}, u32[]{:S(2)}) collective-permute-start(f32[160,128]{1,0:T(8,128)S(1)} %get-tuple-element.19.down_ref), channel_id=1, source_target_pairs={{32,0},{64,32},{96,64},{128,96},{160,128},{192,160},{224,192},{256... | collective-permute-start | bytes 245768 | tf_op jit(solution)/shard_map/ppermute | solution.py:815

commit v4 on v3

--- a/solution.py
+++ b/solution.py
@@ -53,7 +53,7 @@
 LATE_FACE = 3 * SHARE
 EARLY = 16
 RIM_WORDS = 13
-AT_SPEED, AT_POPS, AT_NEXT, AT_MARKS, AT_Z, FACE_ROWS = 0, 12, 68, 88, 152, 160
+AT_SPEED, AT_POPS, AT_NEXT, AT_MARKS, AT_Z, FACE_ROWS = 0, 12, 68, 88, 136, 144
 
 f32 = jnp.float32
 bf16 = jnp.bfloat16
@@ -184,7 +184,8 @@
 
 def spots(base_z):
     count = base_z.shape[1]
-    return jnp.where(iota((LANES, count), 0).astype(f32) == base_z, 1.0, 0.0).astype(bf16)
+    one, none = jnp.ones((), bf16), jnp.zeros((), bf16)
+    return jnp.where(iota((LANES, count), 0).astype(bf16) == base_z.astype(bf16), one, none)
 
 
 def pairs_of(field):
@@ -291,6 +292,7 @@
             )
     rank, rank_up, rank_low = [jnp.concatenate(kind, 1) for kind in ranks]
     rank_ref[...] = rank
+    copies[4].wait()
     lane_up = jnp.where(rank_up < FEW, SLOTS + rank_up, FIRST_SPARE - FEW + rank_up)
     lane_low = jnp.where(
         rank_low < FEW, SLOTS + FEW + rank_low, FIRST_SPARE + SPARE - FEW + rank_low
@@ -312,8 +314,13 @@
     words_z = jnp.where(row.astype(f32) == slot_z, base_z.astype(f32), 0.0)
 
     def to_owners(value, target):
-        rows = [jnp.where(target == number, value, 0.0) for number in range(owners)]
-        return jnp.concatenate(rows, 0).astype(bf16)
+        value = jnp.concatenate([value, value], 0).astype(bf16)
+        target = jnp.broadcast_to(target.astype(f32), (16, markers)).astype(bf16)
+        first = jnp.where(iota((16, markers), 0) < 8, 0.0, 1.0).astype(bf16)
+        rows = []
+        for number in range(0, owners, 2):
+            rows.append(jnp.where(target == first + float(number), value, jnp.zeros((), bf16)))
+        return jnp.concatenate(rows, 0)
 
     def placed(left, spot):
         return lax.dot_general(left, spot, (((1,), (1,)), ((), ())), preferred_element_type=f32)
@@ -324,7 +331,6 @@
     tiles = tiles + placed(to_owners(words_z, owner), spot_z)
     send_ref[...] = tiles.reshape(owners, 8, LANES)
 
-    copies[4].wait()
 
     lane = iota((ROWS, LANES), 1)
     to_right, to_left = jnp.zeros((ROWS, LANES), f32), jnp.zeros((ROWS, LANES), f32)
@@ -364,32 +370,40 @@
     row = iota((ROWS, LANES), 0)
     sources = got_ref.shape[0]
 
-    chosen = iota((LANES, LANES), 1) % SHARE
-    chosen = (iota((LANES, LANES), 0) == FIRST_Z + chosen // 8) & (chosen < SLOTS)
-    every_z = jnp.dot(
-        got_ref[...].reshape(sources * 8, LANES).astype(bf16),
-        chosen.astype(bf16),
-        preferred_element_type=f32,
-    )
-    marks, bases = [], []
-    for tile in range(sources // 4):
-        words, place = None, None
-        for part in range(4):
-            source = tile * 4 + part
-            value = roll(got_ref[source], SHARE * part, 1)
-            spot = every_z[source * 8 : source * 8 + 8, :]
-            if part:
-                words = jnp.where(lane // SHARE == part, value, words)
-                place = jnp.where(lane // SHARE == part, spot, place)
-            else:
-                words, place = value, spot
-        place = jnp.sum(jnp.where(lane % 8 == row, place, 0.0), 0, keepdims=True)
-        place = jnp.where(iota((1, LANES), 1) % SHARE < SLOTS, place, -5.0)
-        marks.append(words)
-        bases.append(place)
-        for ref in (up_ref, down_ref):
-            ref[AT_MARKS + tile * 8 : AT_MARKS + tile * 8 + 8, :] = words
-            ref[AT_Z + tile : AT_Z + tile + 1, :] = place
+    tiles = sources * SLOTS // LANES
+    marks = [None] * tiles
+    twin_marks = [None] * (sources * 2 * FEW // LANES)
+    for source in range(sources):
+        tile, first = divmod(source * SLOTS, LANES)
+        words = roll(got_ref[source], first, 1)
+        marks[tile] = words if marks[tile] is None else jnp.where(lane >= first, words, marks[tile])
+        if first + SLOTS > LANES:
+            marks[tile + 1] = words
+        tile, first = divmod(source * 2 * FEW, LANES)
+        words = roll(got_ref[source], first - SLOTS, 1)
+        old = twin_marks[tile]
+        twin_marks[tile] = words if old is None else jnp.where(lane >= first, words, old)
+    bases = []
+    for tile in range(tiles):
+        first, last = tile * LANES // SLOTS, ((tile + 1) * LANES - 1) // SLOTS
+        rows = jnp.concatenate([got_ref[source] for source in range(first, last + 1)], 0)
+
+        def slot_of(shape):
+            member = iota(shape, 1) + tile * LANES
+            source = (member * 2731) >> 16
+            return source, member - SLOTS * source
+
+        _, slot = slot_of((LANES, LANES))
+        chosen = (iota((LANES, LANES), 0) == FIRST_Z + (slot >> 3)).astype(bf16)
+        value = jnp.dot(rows.astype(bf16), chosen, preferred_element_type=f32)
+        source, slot = slot_of(value.shape)
+        here = iota(value.shape, 0) == (source - first) * 8 + (slot & 7)
+        bases.append(jnp.sum(jnp.where(here, value, 0.0), 0, keepdims=True))
+    for ref in (up_ref, down_ref):
+        for tile in range(tiles):
+            ref[AT_MARKS + tile * 8 : AT_MARKS + tile * 8 + 8, :] = marks[tile]
+            ref[AT_Z + tile : AT_Z + tile + 1, :] = bases[tile]
+        ref[AT_Z + tiles : FACE_ROWS, :] = jnp.zeros((FACE_ROWS - AT_Z - tiles, LANES), f32)
 
     ends = jnp.where(lane >= FIRST_RIM, got_ref[left], roll(got_ref[right], 64, 1))
     rim = [roll(ends, -(FIRST_RIM + PLANES * word), 1) for word in range(RIM_WORDS)]
@@ -419,34 +433,39 @@
         chosen = jnp.where(place < 64, lefts(member).astype(f32), rights(member).astype(f32))
         return chosen.astype(bf16)
 
-    of_left = (lane % SHARE >= SLOTS) & (lane % SHARE < SLOTS + FEW)
-    of_right = lane % SHARE >= SLOTS + FEW
-    near, far = twins(of_left, of_right)
+    near, far = twins(lane % (2 * FEW) < FEW, lane % (2 * FEW) >= FEW)
     side = sides(
-        lambda member: (member % SHARE >= SLOTS) & (member % SHARE < SLOTS + FEW),
-        lambda member: member % SHARE >= SLOTS + FEW,
+        lambda member: member % (2 * FEW) < FEW,
+        lambda member: member % (2 * FEW) >= FEW,
         2 * LANES,
     )
-    of_rim = jnp.zeros((96, LANES), f32)
     rim_left = iota((96, LANES), 1) < 64
     pairs = pairs_of(field_ref[...])
     force = jnp.zeros((96, LANES), f32)
-    for block in range(sources // 8):
+    for block in range(tiles // 2):
         mark = jnp.concatenate(marks[2 * block : 2 * block + 2], 1)
         spot = spots(jnp.concatenate(bases[2 * block : 2 * block + 2], 1))
         found = gathered(pairs, spot)
-        weights = block_weights(mark)
-        here = [found[at * 8 : at * 8 + 8] + jnp.concatenate([near[at]] * 2, 1) for at in range(12)]
-        there = [
-            found[96 + at * 8 : 104 + at * 8] + jnp.concatenate([far[at]] * 2, 1) for at in range(12)
-        ]
-        _, spreads = forces_of(mark, weights, here, there)
+        _, spreads = forces_of(
+            mark,
+            block_weights(mark),
+            [found[at * 8 : at * 8 + 8] for at in range(12)],
+            [found[96 + at * 8 : 104 + at * 8] for at in range(12)],
+        )
         spreads = jnp.concatenate(spreads, 0)
         ahead = spreads * mark[4:5, :]
-        first, second = sums_of(spreads - ahead, ahead, jnp.concatenate([spot, side], 0))
-        force = force + (first[:, 0:LANES] + roll(second[:, 0:LANES], 1, 1))
-        of_rim = of_rim + jnp.where(rim_left, second[:, LANES:], first[:, LANES:])
-    twin_ref[...] = of_rim
+        force = force + scattered(spreads - ahead, ahead, spot)
+    mark = jnp.concatenate(twin_marks, 1)
+    _, spreads = forces_of(
+        mark,
+        block_weights(mark),
+        [jnp.concatenate([value] * 2, 1) for value in near],
+        [jnp.concatenate([value] * 2, 1) for value in far],
+    )
+    spreads = jnp.concatenate(spreads, 0)
+    ahead = spreads * mark[4:5, :]
+    first, second = sums_of(spreads - ahead, ahead, side)
+    twin_ref[...] = jnp.where(rim_left, second, first)
 
     further = jnp.where((lane >= FIRST_SPARE) & (lane < FIRST_Z), 1.0, 0.0)
     most = got_ref[0]
@@ -551,6 +570,7 @@
     lane = iota((ROWS, LANES), 1)
     row = iota((ROWS, LANES), 0)
     sources = back_ref.shape[0]
+    tiles = sources * SLOTS // LANES
 
     def four(ref, at):
         return ref[at : at + PLANES, :]
@@ -597,7 +617,7 @@
     def beyond(ref, field, base_y):
         pairs = pairs_of(jnp.concatenate(field, 0))
         total = jnp.zeros((24, LANES), f32)
-        for block in range(sources // 8):
+        for block in range(tiles // 2):
             tile = AT_MARKS + 16 * block
             mark = jnp.concatenate([ref[tile : tile + 8, :], ref[tile + 8 : tile + 16, :]], 1)
             at = AT_Z + 2 * block
@@ -638,7 +658,7 @@
     pairs = pairs_of(field_ref[...])
     total = jnp.zeros((96, LANES), f32)
     kept = [jnp.zeros((ROWS, LANES), f32) for axis_no in range(3)]
-    for block in range(sources // 8):
+    for block in range(tiles // 2):
         tile = AT_MARKS + 16 * block
         mark = jnp.concatenate([up_ref[tile : tile + 8, :], up_ref[tile + 8 : tile + 16, :]], 1)
         at = AT_Z + 2 * block
@@ -660,14 +680,16 @@
                     row == 2 * block + half, forces[axis_no][:, lanes], kept[axis_no]
                 )
     back_ref[...] = jnp.zeros(back_ref.shape, f32)
-    for part in range(4):
-        value = roll(kept[0], -SHARE * part, 1)
-        for axis_no in range(1, 3):
-            moved = roll(kept[axis_no], SHARE * (axis_no - part), 1)
-            value = jnp.where(lane // SHARE == axis_no, moved, value)
-        for tile in range(sources // 4):
-            back_ref[4 * tile + part, 0:1, :] = value[tile : tile + 1, :]
-
+    following = [roll(value, -1, 0) for value in kept]
+    for part in range(sources // 2):
+        tile, first = divmod(part * SLOTS, LANES)
+        value = None
+        for axis_no in range(3):
+            moved = jnp.where(lane >= first, kept[axis_no], following[axis_no])
+            moved = roll(moved, SHARE * axis_no - first, 1)
+            value = moved if axis_no == 0 else jnp.where(lane // SHARE >= axis_no, moved, value)
+        for source, at in ((part, tile), (part + sources // 2, tile + tiles // 2)):
+            back_ref[source, 0:1, :] = value[at : at + 1, :]
     for plane in range(PLANES):
         ats = [a * 32 + plane * 8 for a in range(3)]
         pops = [wide_ref[member, plane] for member in range(19)]

time: 63.4 us -> 62.5 us (0.986)
  Pallas kernels: 5.77 us -> 4.96 us
    pallas_call x4, Pallas kernels: 5.77 us -> 4.96 us  [call(): pl.pallas_call(kernel, out_shape=out_shape, in_specs=in_specs, out_specs=...]
where the time goes in v4:
time: 62.5 us; the launch traced here: 62.2 us
  blocking collectives  33.6 us (54%)
  starting transfers between devices  20.9 us (33%)
  Pallas kernels  4.96 us (8%)
  waiting for transfers between devices  1.39 us (2%)
  between operations  1.37 us (2%)
    all_to_all x1, blocking collectives, body(): got = lax.all_to_all(send, 'gz', split_axis=0, concat_axis=0, tiled=True)  19.8 us
    ppermute x1, starting transfers between devices, body(): above = lax.ppermute(down, 'gy', [(i + 1, i) for i in range(count_gy - 1)])  16.2 us
    all_to_all x1, blocking collectives, body(): back = lax.all_to_all(back, 'gz', split_axis=0, concat_axis=0, tiled=True)  13.8 us
    pallas_call x4, Pallas kernels, call(): pl.pallas_call(kernel, out_shape=out_shape, in_specs=in_specs, out_specs=...  4.96 us
    ppermute x1, starting transfers between devices, body(): below = lax.ppermute(up, 'gy', [(i, i + 1) for i in range(count_gy - 1)])  4.67 us
  transfers between devices with their start and end apart: 2, of which 2 were waited for; matrix products, arithmetic and copies ran while one was open for 0% of the time, Pallas kernels for 0%

profile of v4, /device:TPU:9, one launch (start us, length us, event | category | flops | bytes accessed | tf_op | source)
XLA Modules:
  0.0 62.2 jit_solution(42384121061833703)
XLA Ops:
  0.6 0.0 copy-start
  1.3 1.7 %shard_map.77 = (f32[32,8,128]{2,1,0:T(8,128)S(1)}, f32[1,512]{1,0:T(1,128)S(1)}, s32[1,512]{1,0:T(1,128)S(1)}, f32[96,128]{1,0:T(8,128)S(1)}, f32[4,8,128]{2,1,0:T(8,128)S(1)}, /*index=5*/f32[4,8,128]{2,1,0:T(8,128)S(1)}) custom-call(s32[1,1]{1,0:T(1,128)} %bitcast.2.count_ref, s32[1,512]{1,0:T(1,128)} %bitcast.3, s32[3,512]{1,0:T(4,128)} %cell_hbm.1, ...), custom_call_target="tpu_custom_call" | custom-call | tf_op jit(solution)/shard_map/pallas_call | solution.py:78
  3.0 19.8 %all_to_all.10.got_ref = f32[32,8,128]{2,1,0:T(8,128)S(1)} all-to-all(f32[32,8,128]{2,1,0:T(8,128)S(1)} %get-tuple-element.13), channel_id=1, replica_groups=mesh['gy'=32,'gz'=32] {'gz'}, dimensions={0} | all-to-all | bytes 262144 | tf_op jit(solution)/shard_map/all_to_all | solution.py:822
  22.8 0.0 copy-done
  22.8 1.1 %shard_map.78 = (f32[19,4,8,128]{3,2,1,0:T(8,128)S(1)}, f32[144,128]{1,0:T(8,128)S(1)}, f32[144,128]{1,0:T(8,128)S(1)}) custom-call(f32[19,4,8,128]{3,2,1,0:T(8,128)S(1)} %copy-done, f32[32,8,128]{2,1,0:T(8,128)S(1)} %all_to_all.10.got_ref, f32[96,128]{1,0:T(8,128)S(1)} %get-tuple-element.14.field_ref, f32[4,8,128]{2,1,0:T(8,128)S(1)} %get-tuple-element.15.density_ref, ...), custom_call_target="tpu_custom_call" | custom-call | tf_op jit(solution)/shard_map/pallas_call | solution.py:78
  23.9 4.7 %collective-permute-start = (f32[144,128]{1,0:T(8,128)S(1)}, f32[144,128]{1,0:T(8,128)S(1)}, u32[]{:S(2)}, u32[]{:S(2)}) collective-permute-start(f32[144,128]{1,0:T(8,128)S(1)} %get-tuple-element.18.up_ref), channel_id=1, source_target_pairs={{0,32},{32,64},{64,96},{96,128},{128,160},{160,192},{192,224},{224... | collective-permute-start | bytes 221192 | tf_op jit(solution)/shard_map/ppermute | solution.py:836
  28.6 16.2 %collective-permute-start.1 = (f32[144,128]{1,0:T(8,128)S(1)}, f32[144,128]{1,0:T(8,128)S(1)}, u32[]{:S(2)}, u32[]{:S(2)}) collective-permute-start(f32[144,128]{1,0:T(8,128)S(1)} %get-tuple-element.19.down_ref), channel_id=1, source_target_pairs={{32,0},{64,32},{96,64},{128,96},{160,128},{192,160},{224,192},{256... | collective-permute-start | bytes 221192 | tf_op jit(solution)/shard_map/ppermute | solution.py:837
  44.8 0.6 collective-permute-done.below_ref
  45.4 0.8 %collective-permute-done.1.above_ref = f32[144,128]{1,0:T(8,128)S(1)} collective-permute-done((f32[144,128]{1,0:T(8,128)S(1)}, f32[144,128]{1,0:T(8,128)S(1)}, u32[]{:S(2)}, u32[]{:S(2)}) %collective-permute-start.1) | collective-permute-done | bytes 73760 | tf_op jit(solution)/shard_map/ppermute | solution.py:837
  46.2 1.3 %shard_map.79 = (f32[19,4,8,128]{3,2,1,0:T(8,128)S(1)}, f32[32,2,128]{2,1,0:T(2,128)S(1)}) custom-call(f32[19,4,8,128]{3,2,1,0:T(8,128)S(1)} %get-tuple-element.17.next_ref, f32[144,128]{1,0:T(8,128)S(1)} %get-tuple-element.18.up_ref, f32[144,128]{1,0:T(8,128)S(1)} %get-tuple-element.19.down_ref, f32[144,128]{1,0:T(8,128)S(1)} %collective-permute-done.below_ref, ...), custom_call_target="tpu_custom_call" | custom-call | tf_op jit(solution)/shard_map/pallas_call | solution.py:78
  47.4 13.8 %all_to_all.11.got_ref = f32[32,2,128]{2,1,0:T(2,128)S(1)} all-to-all(f32[32,2,128]{2,1,0:T(2,128)S(1)} %get-tuple-element.21), channel_id=1, replica_groups=mesh['gy'=32,'gz'=32] {'gz'}, dimensions={0} | all-to-all | bytes 65536 | tf_op jit(solution)/shard_map/all_to_all | solution.py:851
  61.3 1.0 %shard_map.80 = (f32[19,4,8,128]{3,2,1,0:T(8,128)}, f32[3,512]{1,0:T(4,128)}) custom-call(f32[19,4,8,128]{3,2,1,0:T(8,128)S(1)} %get-tuple-element.20.moved_ref, f32[32,2,128]{2,1,0:T(2,128)S(1)} %all_to_all.11.got_ref, s32[1,512]{1,0:T(1,128)S(1)} %get-tuple-element.22.owner_ref, f32[1,512]{1,0:T(1,128)S(1)} %get-tuple-element.23.rank_ref), custom_call_target="tpu_custom_call" | custom-call | tf_op jit(solution)/shard_map/pallas_call | solution.py:78
Async XLA Ops:
  0.6 22.2 %copy-start = (f32[19,4,8,128]{3,2,1,0:T(8,128)S(1)}, f32[19,4,8,128]{3,2,1,0:T(8,128)}, u32[]{:S(2)}) copy-start(f32[19,4,8,128]{3,2,1,0:T(8,128)} %pops_ref.1) | copy-start | bytes 933892
  23.9 21.5 %collective-permute-start = (f32[144,128]{1,0:T(8,128)S(1)}, f32[144,128]{1,0:T(8,128)S(1)}, u32[]{:S(2)}, u32[]{:S(2)}) collective-permute-start(f32[144,128]{1,0:T(8,128)S(1)} %get-tuple-element.18.up_ref), channel_id=1, source_target_pairs={{0,32},{32,64},{64,96},{96,128},{128,160},{160,192},{192,224},{224... | collective-permute-start | bytes 221192 | tf_op jit(solution)/shard_map/ppermute | solution.py:836
  28.6 17.6 %collective-permute-start.1 = (f32[144,128]{1,0:T(8,128)S(1)}, f32[144,128]{1,0:T(8,128)S(1)}, u32[]{:S(2)}, u32[]{:S(2)}) collective-permute-start(f32[144,128]{1,0:T(8,128)S(1)} %get-tuple-element.19.down_ref), channel_id=1, source_target_pairs={{32,0},{64,32},{96,64},{128,96},{160,128},{192,160},{224,192},{256... | collective-permute-start | bytes 221192 | tf_op jit(solution)/shard_map/ppermute | solution.py:837

commit v5 on v4

--- a/solution.py
+++ b/solution.py
@@ -53,7 +53,8 @@
 LATE_FACE = 3 * SHARE
 EARLY = 16
 RIM_WORDS = 13
-AT_SPEED, AT_POPS, AT_NEXT, AT_MARKS, AT_Z, FACE_ROWS = 0, 12, 68, 88, 136, 144
+AT_SPEED, AT_SUMS, AT_POPS, AT_NEXT, AT_MARKS, FACE_ROWS = 0, 12, 36, 56, 80, 128
+AT_Z, MARK_ROWS = 48, 56
 
 f32 = jnp.float32
 bf16 = jnp.bfloat16
@@ -362,7 +363,7 @@
 
 def second_kernel(
     pops_ref, got_ref, field_ref, density_ref, relax_ref,
-    next_ref, up_ref, down_ref,
+    next_ref, up_ref, down_ref, marks_ref,
     post_ref, near_ref, far_ref, twin_ref,
 ):
     left, right = z_neighbours()
@@ -399,11 +400,15 @@
         source, slot = slot_of(value.shape)
         here = iota(value.shape, 0) == (source - first) * 8 + (slot & 7)
         bases.append(jnp.sum(jnp.where(here, value, 0.0), 0, keepdims=True))
+    for tile in range(tiles):
+        marks_ref[tile * 8 : tile * 8 + 8, :] = marks[tile]
+        marks_ref[AT_Z + tile : AT_Z + tile + 1, :] = bases[tile]
+        for ref, base_y in ((up_ref, float(ROWS - 2)), (down_ref, 0.0)):
+            words = jnp.where((row == 0) & (marks[tile][1:2, :] != base_y), 0.0, marks[tile])
+            words = jnp.where(row == 1, bases[tile], words)
+            ref[AT_MARKS + tile * 8 : AT_MARKS + tile * 8 + 8, :] = words
     for ref in (up_ref, down_ref):
-        for tile in range(tiles):
-            ref[AT_MARKS + tile * 8 : AT_MARKS + tile * 8 + 8, :] = marks[tile]
-            ref[AT_Z + tile : AT_Z + tile + 1, :] = bases[tile]
-        ref[AT_Z + tiles : FACE_ROWS, :] = jnp.zeros((FACE_ROWS - AT_Z - tiles, LANES), f32)
+        ref[AT_NEXT + 20 : AT_MARKS, :] = jnp.zeros((AT_MARKS - AT_NEXT - 20, LANES), f32)
 
     ends = jnp.where(lane >= FIRST_RIM, got_ref[left], roll(got_ref[right], 64, 1))
     rim = [roll(ends, -(FIRST_RIM + PLANES * word), 1) for word in range(RIM_WORDS)]
@@ -552,16 +557,31 @@
             at = AT_SPEED + axis_no * PLANES + plane
             up_ref[at : at + 1, :] = speeds[axis_no][ROWS - 2 : ROWS - 1, :]
             down_ref[at : at + 1, :] = speeds[axis_no][1:2, :]
-        for number, member in enumerate(level + rising):
+        cross = pops[11] + pops[12]
+        other = pops[13] + pops[14]
+        across, along = pops[1] + pops[2], pops[5] + pops[6]
+        lean = pops[11] - pops[12]
+        tilt = pops[13] - pops[14]
+        sums = [
+            pops[0] + across + along + cross + other,
+            pops[1] - pops[2] + lean + tilt,
+            pops[5] - pops[6] + lean - tilt,
+            across + cross + other,
+            along + cross + other,
+            cross - other,
+        ]
+        for number, value in enumerate(sums):
+            at = AT_SUMS + number * PLANES + plane
+            up_ref[at : at + 1, :] = value[ROWS - 1 : ROWS, :]
+            down_ref[at : at + 1, :] = value[0:1, :]
+        for number in range(5):
             at = AT_POPS + number * PLANES + plane
-            up_ref[at : at + 1, :] = pops[member][ROWS - 1 : ROWS, :]
-        for number, member in enumerate(level + falling):
-            at = AT_POPS + number * PLANES + plane
-            down_ref[at : at + 1, :] = pops[member][0:1, :]
+            up_ref[at : at + 1, :] = pops[rising[number]][ROWS - 1 : ROWS, :]
+            down_ref[at : at + 1, :] = pops[falling[number]][0:1, :]
 
 
 def third_kernel(
-    next_ref, up_ref, down_ref, below_ref, above_ref,
+    next_ref, up_ref, down_ref, marks_ref, below_ref, above_ref,
     moved_ref, back_ref,
     wide_ref, field_ref, density_ref, post_ref, outer_ref,
 ):
@@ -594,18 +614,24 @@
             field_ref[at : at + 8, :] = speeds[axis_no]
 
     outside = ((row < PLANES) & (first_wall == 0)) | ((row >= PLANES) & (last_wall > 0))
-    outer = []
-    for member in range(19):
-        if member in falling:
-            low = four(down_ref, AT_NEXT + falling.index(member) * PLANES)
-        else:
-            low = four(below_ref, AT_POPS + (level + rising).index(member) * PLANES)
-        if member in rising:
-            top = four(up_ref, AT_NEXT + rising.index(member) * PLANES)
-        else:
-            top = four(above_ref, AT_POPS + (level + falling).index(member) * PLANES)
-        value = jnp.concatenate([low, top], 0)
-        outer.append(jnp.where(outside, 0.0 if member else 1.0, value))
+    sums = []
+    for number in range(6):
+        at = AT_SUMS + number * PLANES
+        sums.append(jnp.concatenate([four(below_ref, at), four(above_ref, at)], 0))
+    half_x, half_z = 0.5 * (sums[3] - sums[5]), 0.5 * (sums[4] - sums[5])
+    nothing = jnp.zeros((ROWS, LANES), f32)
+    outer = [nothing] * 19
+    outer[0] = sums[0] - sums[3] - sums[4] + sums[5]
+    outer[1], outer[2] = half_x + 0.5 * sums[1], half_x - 0.5 * sums[1]
+    outer[5], outer[6] = half_z + 0.5 * sums[2], half_z - 0.5 * sums[2]
+    outer[11] = outer[12] = 0.5 * sums[5]
+    for number in range(5):
+        known, mine = AT_POPS + number * PLANES, AT_NEXT + number * PLANES
+        outer[rising[number]] = jnp.concatenate([four(below_ref, known), four(up_ref, mine)], 0)
+        outer[falling[number]] = jnp.concatenate([four(down_ref, mine), four(above_ref, known)], 0)
+    outer = [
+        jnp.where(outside, 0.0 if member else 1.0, value) for member, value in enumerate(outer)
+    ]
     outer_density, outer_speeds = moments_of(outer)
     lows, tops = [], []
     for axis_no in range(3):
@@ -614,21 +640,18 @@
         lows.append(jnp.where(row < PLANES, outer_speeds[axis_no], second))
         tops.append(jnp.where(row < PLANES, second, outer_speeds[axis_no]))
 
-    def beyond(ref, field, base_y):
+    def beyond(ref, field):
         pairs = pairs_of(jnp.concatenate(field, 0))
         total = jnp.zeros((24, LANES), f32)
         for block in range(tiles // 2):
             tile = AT_MARKS + 16 * block
             mark = jnp.concatenate([ref[tile : tile + 8, :], ref[tile + 8 : tile + 16, :]], 1)
-            at = AT_Z + 2 * block
-            base = jnp.concatenate([ref[at : at + 1, :], ref[at + 1 : at + 2, :]], 1)
-            spot = spots(base)
+            spot = spots(mark[1:2, :])
             found = gathered(pairs, spot)
             place = iota((ROWS, 2 * LANES), 0)
             frac = mark[3:4, :]
             weight = along_x(mark, (place % PLANES).astype(f32))
             weight = weight * jnp.where(place < PLANES, frac, 1.0 - frac)
-            weight = jnp.where(mark[1:2, :] == base_y, weight, 0.0)
             frac = mark[4:5, :]
             spreads = []
             for axis_no in range(3):
@@ -642,8 +665,8 @@
             total = total + scattered(spreads - ahead, ahead, spot)
         return total
 
-    from_below = beyond(below_ref, lows, float(ROWS - 2))
-    from_above = beyond(above_ref, tops, 0.0)
+    from_below = beyond(below_ref, lows)
+    from_above = beyond(above_ref, tops)
     outer_pulls = [
         jnp.where(row < PLANES, from_below[a * 8 : a * 8 + 8], from_above[a * 8 : a * 8 + 8])
         for a in range(3)
@@ -659,10 +682,10 @@
     total = jnp.zeros((96, LANES), f32)
     kept = [jnp.zeros((ROWS, LANES), f32) for axis_no in range(3)]
     for block in range(tiles // 2):
-        tile = AT_MARKS + 16 * block
-        mark = jnp.concatenate([up_ref[tile : tile + 8, :], up_ref[tile + 8 : tile + 16, :]], 1)
+        tile = 16 * block
+        mark = jnp.concatenate([marks_ref[tile : tile + 8, :], marks_ref[tile + 8 : tile + 16, :]], 1)
         at = AT_Z + 2 * block
-        spot = spots(jnp.concatenate([up_ref[at : at + 1, :], up_ref[at + 1 : at + 2, :]], 1))
+        spot = spots(jnp.concatenate([marks_ref[at : at + 1, :], marks_ref[at + 1 : at + 2, :]], 1))
         found = gathered(pairs, spot)
         forces, spreads = forces_of(
             mark,
@@ -821,9 +844,9 @@
     )
     got = lax.all_to_all(send, "gz", split_axis=0, concat_axis=0, tiled=True)
     face = shape((FACE_ROWS, LANES), f32)
-    next_pops, up, down = call(
+    next_pops, up, down, marks = call(
         second_kernel,
-        [lattice, face, face],
+        [lattice, face, face, shape((MARK_ROWS, LANES), f32)],
         [populations, got, speeds, density, relax],
         [vmem] * 5,
         scratch=[
@@ -838,8 +861,8 @@
     moved, back = call(
         third_kernel,
         [lattice, shape((count_gz, 2, LANES), f32)],
-        [next_pops, up, down, below, above],
-        [vmem] * 5,
+        [next_pops, up, down, marks, below, above],
+        [vmem] * 6,
         scratch=[
             pltpu.VMEM(populations.shape, f32),
             pltpu.VMEM((96, LANES), f32),

time: 62.5 us -> 62.4 us (level)
  no operation moved by 1% of the time
where the time goes in v5:
time: 62.4 us; the launch traced here: 62.2 us
  blocking collectives  33.6 us (54%)
  starting transfers between devices  20.9 us (33%)
  Pallas kernels  4.97 us (8%)
  between operations  1.37 us (2%)
  waiting for transfers between devices  1.31 us (2%)
    all_to_all x1, blocking collectives, body(): got = lax.all_to_all(send, 'gz', split_axis=0, concat_axis=0, tiled=True)  19.8 us
    ppermute x1, starting transfers between devices, body(): above = lax.ppermute(down, 'gy', [(i + 1, i) for i in range(count_gy - 1)])  16.2 us
    all_to_all x1, blocking collectives, body(): back = lax.all_to_all(back, 'gz', split_axis=0, concat_axis=0, tiled=True)  13.8 us
    pallas_call x4, Pallas kernels, call(): pl.pallas_call(kernel, out_shape=out_shape, in_specs=in_specs, out_specs=...  4.97 us
    ppermute x1, starting transfers between devices, body(): below = lax.ppermute(up, 'gy', [(i, i + 1) for i in range(count_gy - 1)])  4.67 us
  transfers between devices with their start and end apart: 2, of which 2 were waited for; matrix products, arithmetic and copies ran while one was open for 0% of the time, Pallas kernels for 0%

profile of v5, /device:TPU:9, one launch (start us, length us, event | category | flops | bytes accessed | tf_op | source)
XLA Modules:
  0.0 62.2 jit_solution(5637741401222839023)
XLA Ops:
  0.6 0.0 copy-start
  1.3 1.7 %shard_map.77 = (f32[32,8,128]{2,1,0:T(8,128)S(1)}, f32[1,512]{1,0:T(1,128)S(1)}, s32[1,512]{1,0:T(1,128)S(1)}, f32[96,128]{1,0:T(8,128)S(1)}, f32[4,8,128]{2,1,0:T(8,128)S(1)}, /*index=5*/f32[4,8,128]{2,1,0:T(8,128)S(1)}) custom-call(s32[1,1]{1,0:T(1,128)} %bitcast.2.count_ref, s32[1,512]{1,0:T(1,128)} %bitcast.3, s32[3,512]{1,0:T(4,128)} %cell_hbm.1, ...), custom_call_target="tpu_custom_call" | custom-call | tf_op jit(solution)/shard_map/pallas_call | solution.py:79
  3.0 19.8 %all_to_all.10.got_ref = f32[32,8,128]{2,1,0:T(8,128)S(1)} all-to-all(f32[32,8,128]{2,1,0:T(8,128)S(1)} %get-tuple-element.14), channel_id=1, replica_groups=mesh['gy'=32,'gz'=32] {'gz'}, dimensions={0} | all-to-all | bytes 262144 | tf_op jit(solution)/shard_map/all_to_all | solution.py:845
  22.8 0.0 copy-done
  22.8 1.1 %shard_map.78 = (f32[19,4,8,128]{3,2,1,0:T(8,128)S(1)}, f32[128,128]{1,0:T(8,128)S(1)}, f32[128,128]{1,0:T(8,128)S(1)}, f32[56,128]{1,0:T(8,128)S(1)}) custom-call(f32[19,4,8,128]{3,2,1,0:T(8,128)S(1)} %copy-done, f32[32,8,128]{2,1,0:T(8,128)S(1)} %all_to_all.10.got_ref, f32[96,128]{1,0:T(8,128)S(1)} %get-tuple-element.15.field_ref, ...), custom_call_target="tpu_custom_call" | custom-call | tf_op jit(solution)/shard_map/pallas_call | solution.py:79
  23.9 4.7 %collective-permute-start = (f32[128,128]{1,0:T(8,128)S(1)}, f32[128,128]{1,0:T(8,128)S(1)}, u32[]{:S(2)}, u32[]{:S(2)}) collective-permute-start(f32[128,128]{1,0:T(8,128)S(1)} %get-tuple-element.19.up_ref), channel_id=1, source_target_pairs={{0,32},{32,64},{64,96},{96,128},{128,160},{160,192},{192,224},{224... | collective-permute-start | bytes 196616 | tf_op jit(solution)/shard_map/ppermute | solution.py:859
  28.6 16.2 %collective-permute-start.1 = (f32[128,128]{1,0:T(8,128)S(1)}, f32[128,128]{1,0:T(8,128)S(1)}, u32[]{:S(2)}, u32[]{:S(2)}) collective-permute-start(f32[128,128]{1,0:T(8,128)S(1)} %get-tuple-element.20.down_ref), channel_id=1, source_target_pairs={{32,0},{64,32},{96,64},{128,96},{160,128},{192,160},{224,192},{256... | collective-permute-start | bytes 196616 | tf_op jit(solution)/shard_map/ppermute | solution.py:860
  44.8 0.4 collective-permute-done.below_ref
  45.2 0.9 %collective-permute-done.1.above_ref = f32[128,128]{1,0:T(8,128)S(1)} collective-permute-done((f32[128,128]{1,0:T(8,128)S(1)}, f32[128,128]{1,0:T(8,128)S(1)}, u32[]{:S(2)}, u32[]{:S(2)}) %collective-permute-start.1) | collective-permute-done | bytes 65568 | tf_op jit(solution)/shard_map/ppermute | solution.py:860
  46.1 1.3 %shard_map.79 = (f32[19,4,8,128]{3,2,1,0:T(8,128)S(1)}, f32[32,2,128]{2,1,0:T(2,128)S(1)}) custom-call(f32[19,4,8,128]{3,2,1,0:T(8,128)S(1)} %get-tuple-element.18.next_ref, f32[128,128]{1,0:T(8,128)S(1)} %get-tuple-element.19.up_ref, f32[128,128]{1,0:T(8,128)S(1)} %get-tuple-element.20.down_ref, f32[56,128]{1,0:T(8,128)S(1)} %get-tuple-element.21.marks_ref, ...), custom_call_target="tpu_custom_call" | custom-call | tf_op jit(solution)/shard_map/pallas_call | solution.py:79
  47.4 13.8 %all_to_all.11.got_ref = f32[32,2,128]{2,1,0:T(2,128)S(1)} all-to-all(f32[32,2,128]{2,1,0:T(2,128)S(1)} %get-tuple-element.23), channel_id=1, replica_groups=mesh['gy'=32,'gz'=32] {'gz'}, dimensions={0} | all-to-all | bytes 65536 | tf_op jit(solution)/shard_map/all_to_all | solution.py:874
  61.2 1.0 %shard_map.80 = (f32[19,4,8,128]{3,2,1,0:T(8,128)}, f32[3,512]{1,0:T(4,128)}) custom-call(f32[19,4,8,128]{3,2,1,0:T(8,128)S(1)} %get-tuple-element.22.moved_ref, f32[32,2,128]{2,1,0:T(2,128)S(1)} %all_to_all.11.got_ref, s32[1,512]{1,0:T(1,128)S(1)} %get-tuple-element.24.owner_ref, f32[1,512]{1,0:T(1,128)S(1)} %get-tuple-element.25.rank_ref), custom_call_target="tpu_custom_call" | custom-call | tf_op jit(solution)/shard_map/pallas_call | solution.py:79
Async XLA Ops:
  0.6 22.2 %copy-start = (f32[19,4,8,128]{3,2,1,0:T(8,128)S(1)}, f32[19,4,8,128]{3,2,1,0:T(8,128)}, u32[]{:S(2)}) copy-start(f32[19,4,8,128]{3,2,1,0:T(8,128)} %pops_ref.1) | copy-start | bytes 933892
  23.9 21.3 %collective-permute-start = (f32[128,128]{1,0:T(8,128)S(1)}, f32[128,128]{1,0:T(8,128)S(1)}, u32[]{:S(2)}, u32[]{:S(2)}) collective-permute-start(f32[128,128]{1,0:T(8,128)S(1)} %get-tuple-element.19.up_ref), channel_id=1, source_target_pairs={{0,32},{32,64},{64,96},{96,128},{128,160},{160,192},{192,224},{224... | collective-permute-start | bytes 196616 | tf_op jit(solution)/shard_map/ppermute | solution.py:859
  28.6 17.5 %collective-permute-start.1 = (f32[128,128]{1,0:T(8,128)S(1)}, f32[128,128]{1,0:T(8,128)S(1)}, u32[]{:S(2)}, u32[]{:S(2)}) collective-permute-start(f32[128,128]{1,0:T(8,128)S(1)} %get-tuple-element.20.down_ref), channel_id=1, source_target_pairs={{32,0},{64,32},{96,64},{128,96},{160,128},{192,160},{224,192},{256... | collective-permute-start | bytes 196616 | tf_op jit(solution)/shard_map/ppermute | solution.py:860

commit v6 on v5

--- a/solution.py
+++ b/solution.py
@@ -239,8 +239,8 @@
 
 def first_kernel(
     count_ref, owner_hbm, cell_hbm, frac_hbm, speed_hbm, pops_hbm,
-    send_ref, rank_ref, live_ref, field_ref, density_ref, relax_ref,
-    owner_ref, cell_ref, frac_ref, speed_ref, pops_ref, sems,
+    send_ref, rank_ref, live_ref, pops_ref, field_ref, density_ref, relax_ref,
+    owner_ref, cell_ref, frac_ref, speed_ref, sems,
 ):
     copies = [
         pltpu.make_async_copy(source, target, sems.at[number])
@@ -833,13 +833,21 @@
         marker_speed,
         populations,
     ]
-    send, rank, live, speeds, density, relax = call(
+    send, rank, live, held, speeds, density, relax = call(
         first_kernel,
-        [tiles, shape((1, markers), f32), shape((1, markers), jnp.int32), field, cells, cells],
+        [
+            tiles,
+            shape((1, markers), f32),
+            shape((1, markers), jnp.int32),
+            lattice,
+            field,
+            cells,
+            cells,
+        ],
         [marker_count.reshape(1, 1)]
         + [pltpu.with_memory_space_constraint(value, pltpu.HBM) for value in inputs],
         [vmem] + [pl.BlockSpec(memory_space=pltpu.HBM)] * 5,
-        scratch=[pltpu.VMEM(value.shape, value.dtype) for value in inputs]
+        scratch=[pltpu.VMEM(value.shape, value.dtype) for value in inputs[0:4]]
         + [pltpu.SemaphoreType.DMA((5,))],
     )
     got = lax.all_to_all(send, "gz", split_axis=0, concat_axis=0, tiled=True)
@@ -847,7 +855,7 @@
     next_pops, up, down, marks = call(
         second_kernel,
         [lattice, face, face, shape((MARK_ROWS, LANES), f32)],
-        [populations, got, speeds, density, relax],
+        [held, got, speeds, density, relax],
         [vmem] * 5,
         scratch=[
             pltpu.VMEM(populations.shape, f32),

time: 62.4 us -> 62.4 us (level)
  no operation moved by 1% of the time
where the time goes in v6:
time: 62.4 us; the launch traced here: 62.1 us
  blocking collectives  33.6 us (54%)
  starting transfers between devices  20.9 us (33%)
  Pallas kernels  4.98 us (8%)
  between operations  1.32 us (2%)
  waiting for transfers between devices  1.31 us (2%)
    all_to_all x1, blocking collectives, body(): got = lax.all_to_all(send, 'gz', split_axis=0, concat_axis=0, tiled=True)  19.8 us
    ppermute x1, starting transfers between devices, body(): above = lax.ppermute(down, 'gy', [(i + 1, i) for i in range(count_gy - 1)])  16.2 us
    all_to_all x1, blocking collectives, body(): back = lax.all_to_all(back, 'gz', split_axis=0, concat_axis=0, tiled=True)  13.8 us
    pallas_call x4, Pallas kernels, call(): pl.pallas_call(kernel, out_shape=out_shape, in_specs=in_specs, out_specs=...  4.98 us
    ppermute x1, starting transfers between devices, body(): below = lax.ppermute(up, 'gy', [(i, i + 1) for i in range(count_gy - 1)])  4.67 us
  transfers between devices with their start and end apart: 2, of which 2 were waited for; matrix products, arithmetic and copies ran while one was open for 0% of the time, Pallas kernels for 0%

profile of v6, /device:TPU:9, one launch (start us, length us, event | category | flops | bytes accessed | tf_op | source)
XLA Modules:
  0.0 62.1 jit_solution(17682565970425553531)
XLA Ops:
  1.3 1.7 %shard_map.77 = (f32[32,8,128]{2,1,0:T(8,128)S(1)}, f32[1,512]{1,0:T(1,128)S(1)}, s32[1,512]{1,0:T(1,128)S(1)}, f32[19,4,8,128]{3,2,1,0:T(8,128)S(1)}, f32[96,12...) custom-call(s32[1,1]{1,0:T(1,128)} %bitcast.2.count_ref, s32[1,512]{1,0:T(1,128)} %bitcast.3, ...), custom_call_target="tpu_custom_call" | custom-call | tf_op jit(solution)/shard_map/pallas_call | solution.py:79
  3.0 19.8 %all_to_all.10.got_ref = f32[32,8,128]{2,1,0:T(8,128)S(1)} all-to-all(f32[32,8,128]{2,1,0:T(8,128)S(1)} %get-tuple-element.16), channel_id=1, replica_groups=mesh['gy'=32,'gz'=32] {'gz'}, dimensions={0} | all-to-all | bytes 262144 | tf_op jit(solution)/shard_map/all_to_all | solution.py:853
  22.8 1.1 %shard_map.78 = (f32[19,4,8,128]{3,2,1,0:T(8,128)S(1)}, f32[128,128]{1,0:T(8,128)S(1)}, f32[128,128]{1,0:T(8,128)S(1)}, f32[56,128]{1,0:T(8,128)S(1)}) custom-call(f32[19,4,8,128]{3,2,1,0:T(8,128)S(1)} %get-tuple-element.15.pops_ref, f32[32,8,128]{2,1,0:T(8,128)S(1)} %all_to_all.10.got_ref, f32[96,128]{1,0:T(8,128)S(1)} %get-tuple-element.17.field_ref, ...), custom_call_target="tpu_custom_call" | custom-call | tf_op jit(solution)/shard_map/pallas_call | solution.py:79
  23.9 4.7 %collective-permute-start = (f32[128,128]{1,0:T(8,128)S(1)}, f32[128,128]{1,0:T(8,128)S(1)}, u32[]{:S(2)}, u32[]{:S(2)}) collective-permute-start(f32[128,128]{1,0:T(8,128)S(1)} %get-tuple-element.21.up_ref), channel_id=1, source_target_pairs={{0,32},{32,64},{64,96},{96,128},{128,160},{160,192},{192,224},{224... | collective-permute-start | bytes 196616 | tf_op jit(solution)/shard_map/ppermute | solution.py:867
  28.5 16.2 %collective-permute-start.1 = (f32[128,128]{1,0:T(8,128)S(1)}, f32[128,128]{1,0:T(8,128)S(1)}, u32[]{:S(2)}, u32[]{:S(2)}) collective-permute-start(f32[128,128]{1,0:T(8,128)S(1)} %get-tuple-element.22.down_ref), channel_id=1, source_target_pairs={{32,0},{64,32},{96,64},{128,96},{160,128},{192,160},{224,192},{256... | collective-permute-start | bytes 196616 | tf_op jit(solution)/shard_map/ppermute | solution.py:868
  44.8 0.4 collective-permute-done.below_ref
  45.2 0.9 %collective-permute-done.1.above_ref = f32[128,128]{1,0:T(8,128)S(1)} collective-permute-done((f32[128,128]{1,0:T(8,128)S(1)}, f32[128,128]{1,0:T(8,128)S(1)}, u32[]{:S(2)}, u32[]{:S(2)}) %collective-permute-start.1) | collective-permute-done | bytes 65568 | tf_op jit(solution)/shard_map/ppermute | solution.py:868
  46.1 1.3 %shard_map.79 = (f32[19,4,8,128]{3,2,1,0:T(8,128)S(1)}, f32[32,2,128]{2,1,0:T(2,128)S(1)}) custom-call(f32[19,4,8,128]{3,2,1,0:T(8,128)S(1)} %get-tuple-element.20.next_ref, f32[128,128]{1,0:T(8,128)S(1)} %get-tuple-element.21.up_ref, f32[128,128]{1,0:T(8,128)S(1)} %get-tuple-element.22.down_ref, f32[56,128]{1,0:T(8,128)S(1)} %get-tuple-element.23.marks_ref, ...), custom_call_target="tpu_custom_call" | custom-call | tf_op jit(solution)/shard_map/pallas_call | solution.py:79
  47.3 13.8 %all_to_all.11.got_ref = f32[32,2,128]{2,1,0:T(2,128)S(1)} all-to-all(f32[32,2,128]{2,1,0:T(2,128)S(1)} %get-tuple-element.25), channel_id=1, replica_groups=mesh['gy'=32,'gz'=32] {'gz'}, dimensions={0} | all-to-all | bytes 65536 | tf_op jit(solution)/shard_map/all_to_all | solution.py:882
  61.2 1.0 %shard_map.80 = (f32[19,4,8,128]{3,2,1,0:T(8,128)}, f32[3,512]{1,0:T(4,128)}) custom-call(f32[19,4,8,128]{3,2,1,0:T(8,128)S(1)} %get-tuple-element.24.moved_ref, f32[32,2,128]{2,1,0:T(2,128)S(1)} %all_to_all.11.got_ref, s32[1,512]{1,0:T(1,128)S(1)} %get-tuple-element.26.owner_ref, f32[1,512]{1,0:T(1,128)S(1)} %get-tuple-element.27.rank_ref), custom_call_target="tpu_custom_call" | custom-call | tf_op jit(solution)/shard_map/pallas_call | solution.py:79
Async XLA Ops:
  23.9 21.3 %collective-permute-start = (f32[128,128]{1,0:T(8,128)S(1)}, f32[128,128]{1,0:T(8,128)S(1)}, u32[]{:S(2)}, u32[]{:S(2)}) collective-permute-start(f32[128,128]{1,0:T(8,128)S(1)} %get-tuple-element.21.up_ref), channel_id=1, source_target_pairs={{0,32},{32,64},{64,96},{96,128},{128,160},{160,192},{192,224},{224... | collective-permute-start | bytes 196616 | tf_op jit(solution)/shard_map/ppermute | solution.py:867
  28.5 17.5 %collective-permute-start.1 = (f32[128,128]{1,0:T(8,128)S(1)}, f32[128,128]{1,0:T(8,128)S(1)}, u32[]{:S(2)}, u32[]{:S(2)}) collective-permute-start(f32[128,128]{1,0:T(8,128)S(1)} %get-tuple-element.22.down_ref), channel_id=1, source_target_pairs={{32,0},{64,32},{96,64},{128,96},{160,128},{192,160},{224,192},{256... | collective-permute-start | bytes 196616 | tf_op jit(solution)/shard_map/ppermute | solution.py:868

commit v7 on v6

--- a/solution.py
+++ b/solution.py
@@ -134,7 +134,7 @@
     xz = pair[5] - pair[6] - moved[0] * speeds[2]
     yz = pair[7] - pair[8] - moved[1] * speeds[2]
     norm_sq = xx * xx + yy * yy + zz * zz + 2.0 * (xy * xy + xz * xz + yz * yz)
-    return 0.5 * (tau_base + jnp.sqrt(tau_base * tau_base + factor * jnp.sqrt(norm_sq) / density))
+    return 0.5 * (tau_base + jnp.sqrt(tau_base * tau_base + factor * jnp.sqrt(norm_sq) * (1.0 / density)))
 
 
 def along_of(member, speeds):
@@ -149,7 +149,7 @@
 
 
 def relaxed(pops, density, speeds, relax, pulls):
-    pull = relax / density
+    pull = relax * (1.0 / density)
     shifted = [speeds[a] + pull * pulls[a] for a in range(3)]
     shifted_sq = shifted[0] * shifted[0] + shifted[1] * shifted[1] + shifted[2] * shifted[2]
     rate = 1.0 / relax

time: 62.4 us -> 62.4 us (level)
  no operation moved by 1% of the time
where the time goes in v7:
time: 62.4 us; the launch traced here: 62.1 us
  blocking collectives  33.6 us (54%)
  starting transfers between devices  20.9 us (33%)
  Pallas kernels  4.98 us (8%)
  between operations  1.32 us (2%)
  waiting for transfers between devices  1.31 us (2%)
    all_to_all x1, blocking collectives, body(): got = lax.all_to_all(send, 'gz', split_axis=0, concat_axis=0, tiled=True)  19.8 us
    ppermute x1, starting transfers between devices, body(): above = lax.ppermute(down, 'gy', [(i + 1, i) for i in range(count_gy - 1)])  16.2 us
    all_to_all x1, blocking collectives, body(): back = lax.all_to_all(back, 'gz', split_axis=0, concat_axis=0, tiled=True)  13.8 us
    pallas_call x4, Pallas kernels, call(): pl.pallas_call(kernel, out_shape=out_shape, in_specs=in_specs, out_specs=...  4.98 us
    ppermute x1, starting transfers between devices, body(): below = lax.ppermute(up, 'gy', [(i, i + 1) for i in range(count_gy - 1)])  4.67 us
  transfers between devices with their start and end apart: 2, of which 2 were waited for; matrix products, arithmetic and copies ran while one was open for 0% of the time, Pallas kernels for 0%

profile of v7, /device:TPU:9, one launch (start us, length us, event | category | flops | bytes accessed | tf_op | source)
XLA Modules:
  0.0 62.1 jit_solution(17682565970425553531)
XLA Ops:
  1.3 1.7 %shard_map.77 = (f32[32,8,128]{2,1,0:T(8,128)S(1)}, f32[1,512]{1,0:T(1,128)S(1)}, s32[1,512]{1,0:T(1,128)S(1)}, f32[19,4,8,128]{3,2,1,0:T(8,128)S(1)}, f32[96,12...) custom-call(s32[1,1]{1,0:T(1,128)} %bitcast.2.count_ref, s32[1,512]{1,0:T(1,128)} %bitcast.3, ...), custom_call_target="tpu_custom_call" | custom-call | tf_op jit(solution)/shard_map/pallas_call | solution.py:79
  3.0 19.8 %all_to_all.10.got_ref = f32[32,8,128]{2,1,0:T(8,128)S(1)} all-to-all(f32[32,8,128]{2,1,0:T(8,128)S(1)} %get-tuple-element.16), channel_id=1, replica_groups=mesh['gy'=32,'gz'=32] {'gz'}, dimensions={0} | all-to-all | bytes 262144 | tf_op jit(solution)/shard_map/all_to_all | solution.py:853
  22.8 1.1 %shard_map.78 = (f32[19,4,8,128]{3,2,1,0:T(8,128)S(1)}, f32[128,128]{1,0:T(8,128)S(1)}, f32[128,128]{1,0:T(8,128)S(1)}, f32[56,128]{1,0:T(8,128)S(1)}) custom-call(f32[19,4,8,128]{3,2,1,0:T(8,128)S(1)} %get-tuple-element.15.pops_ref, f32[32,8,128]{2,1,0:T(8,128)S(1)} %all_to_all.10.got_ref, f32[96,128]{1,0:T(8,128)S(1)} %get-tuple-element.17.field_ref, ...), custom_call_target="tpu_custom_call" | custom-call | tf_op jit(solution)/shard_map/pallas_call | solution.py:79
  23.9 4.7 %collective-permute-start = (f32[128,128]{1,0:T(8,128)S(1)}, f32[128,128]{1,0:T(8,128)S(1)}, u32[]{:S(2)}, u32[]{:S(2)}) collective-permute-start(f32[128,128]{1,0:T(8,128)S(1)} %get-tuple-element.21.up_ref), channel_id=1, source_target_pairs={{0,32},{32,64},{64,96},{96,128},{128,160},{160,192},{192,224},{224... | collective-permute-start | bytes 196616 | tf_op jit(solution)/shard_map/ppermute | solution.py:867
  28.5 16.2 %collective-permute-start.1 = (f32[128,128]{1,0:T(8,128)S(1)}, f32[128,128]{1,0:T(8,128)S(1)}, u32[]{:S(2)}, u32[]{:S(2)}) collective-permute-start(f32[128,128]{1,0:T(8,128)S(1)} %get-tuple-element.22.down_ref), channel_id=1, source_target_pairs={{32,0},{64,32},{96,64},{128,96},{160,128},{192,160},{224,192},{256... | collective-permute-start | bytes 196616 | tf_op jit(solution)/shard_map/ppermute | solution.py:868
  44.8 0.4 collective-permute-done.below_ref
  45.2 0.9 %collective-permute-done.1.above_ref = f32[128,128]{1,0:T(8,128)S(1)} collective-permute-done((f32[128,128]{1,0:T(8,128)S(1)}, f32[128,128]{1,0:T(8,128)S(1)}, u32[]{:S(2)}, u32[]{:S(2)}) %collective-permute-start.1) | collective-permute-done | bytes 65568 | tf_op jit(solution)/shard_map/ppermute | solution.py:868
  46.1 1.3 %shard_map.79 = (f32[19,4,8,128]{3,2,1,0:T(8,128)S(1)}, f32[32,2,128]{2,1,0:T(2,128)S(1)}) custom-call(f32[19,4,8,128]{3,2,1,0:T(8,128)S(1)} %get-tuple-element.20.next_ref, f32[128,128]{1,0:T(8,128)S(1)} %get-tuple-element.21.up_ref, f32[128,128]{1,0:T(8,128)S(1)} %get-tuple-element.22.down_ref, f32[56,128]{1,0:T(8,128)S(1)} %get-tuple-element.23.marks_ref, ...), custom_call_target="tpu_custom_call" | custom-call | tf_op jit(solution)/shard_map/pallas_call | solution.py:79
  47.3 13.8 %all_to_all.11.got_ref = f32[32,2,128]{2,1,0:T(2,128)S(1)} all-to-all(f32[32,2,128]{2,1,0:T(2,128)S(1)} %get-tuple-element.25), channel_id=1, replica_groups=mesh['gy'=32,'gz'=32] {'gz'}, dimensions={0} | all-to-all | bytes 65536 | tf_op jit(solution)/shard_map/all_to_all | solution.py:882
  61.2 1.0 %shard_map.80 = (f32[19,4,8,128]{3,2,1,0:T(8,128)}, f32[3,512]{1,0:T(4,128)}) custom-call(f32[19,4,8,128]{3,2,1,0:T(8,128)S(1)} %get-tuple-element.24.moved_ref, f32[32,2,128]{2,1,0:T(2,128)S(1)} %all_to_all.11.got_ref, s32[1,512]{1,0:T(1,128)S(1)} %get-tuple-element.26.owner_ref, f32[1,512]{1,0:T(1,128)S(1)} %get-tuple-element.27.rank_ref), custom_call_target="tpu_custom_call" | custom-call | tf_op jit(solution)/shard_map/pallas_call | solution.py:79
Async XLA Ops:
  23.9 21.3 %collective-permute-start = (f32[128,128]{1,0:T(8,128)S(1)}, f32[128,128]{1,0:T(8,128)S(1)}, u32[]{:S(2)}, u32[]{:S(2)}) collective-permute-start(f32[128,128]{1,0:T(8,128)S(1)} %get-tuple-element.21.up_ref), channel_id=1, source_target_pairs={{0,32},{32,64},{64,96},{96,128},{128,160},{160,192},{192,224},{224... | collective-permute-start | bytes 196616 | tf_op jit(solution)/shard_map/ppermute | solution.py:867
  28.5 17.5 %collective-permute-start.1 = (f32[128,128]{1,0:T(8,128)S(1)}, f32[128,128]{1,0:T(8,128)S(1)}, u32[]{:S(2)}, u32[]{:S(2)}) collective-permute-start(f32[128,128]{1,0:T(8,128)S(1)} %get-tuple-element.22.down_ref), channel_id=1, source_target_pairs={{32,0},{64,32},{96,64},{128,96},{160,128},{192,160},{224,192},{256... | collective-permute-start | bytes 196616 | tf_op jit(solution)/shard_map/ppermute | solution.py:868
